TPU v7x, 256 devices: a whole 4x4x8 slice. The times are simulated.
256 devices in a mesh: ctx: 64 (over y, z, core), mp: 4 (over x).
Axes of the slice: x: 4, y: 4, z: 8, core: 2. Of those that a mesh axis runs over, the one named last changes fastest.
Arguments:
- query: bfloat16 [256, 8, 8, 128], P(('ctx', 'mp')), may hold values from -8 to 8
- keys: bfloat16 [256, 8, 2048, 128], P(('ctx', 'mp')), may hold values from -5 to 5
- values: bfloat16 [256, 8, 2048, 128], P(('ctx', 'mp')), may hold values from -6 to 6
- chosen: int32 [8, 256, 16], replicated, may hold values from 0 to 255, all different within a row; in each aligned block of 256 rows (0 to 255, 256 to 511, ..., all dimensions but the last counted through in order) at most 64 rows name the same one
- residual: bfloat16 [256, 8192], P('ctx', 'mp'), may hold values from -1.5 to 1.5
- output_weight: bfloat16 [8192, 8192], P('ctx', 'mp'), may hold values from -0.0625 to 0.0625
- norm_gain: float32 [8192], P('mp'), may hold values from 0.5 to 1.5
- gate_weight: bfloat16 [8192, 14336], P('mp', 'ctx'), may hold values from -0.0625 to 0.0625
- up_weight: bfloat16 [8192, 14336], P('mp', 'ctx'), may hold values from -0.0625 to 0.0625
- down_weight: bfloat16 [14336, 8192], P('ctx', 'mp'), may hold values from -0.046875 to 0.046875
Outputs:
- stream: bfloat16 [256, 8192], P('ctx', 'mp')
- update: bfloat16 [256, 8192], P('ctx', 'mp')
Inputs may be any that keep to these rules, and one draw needn't show every extreme that they name: `chosen`: for each KV head, each row lists 16 different partitions; no partition is listed by more than 64 rows of one KV head, and in every draw some partition is listed by exactly 64 rows of some KV head.
All inputs are finite; a program needn't handle non-finite values.
Results may differ from a plain program's by a relative error of at most 0.025.
Values may be sent and summed in bfloat16 or wider, within the bound.
A program may use at most 128 MiB of HBM per device.

v0:
```python
import jax
import jax.numpy as jnp
from jax import lax
from jax.sharding import PartitionSpec as P

MODEL_WIDTH = 8192
KEPT_PARTITIONS = 16
ROW_DEV = 1


norm_eps = 1e-05
lowest_value = -1e30


def find_slots(listed, target, capacity):
    member = jnp.any(listed == target, axis=2)
    places = jnp.cumsum(member.astype(jnp.int32), axis=1) - 1
    live_count = jnp.sum(member.astype(jnp.int32), axis=1)
    slot_ranks = jnp.arange(capacity, dtype=jnp.int32)
    slot_hits = member[:, :, None] & (places[:, :, None] == slot_ranks[None, None, :])
    row_numbers = jnp.arange(listed.shape[1], dtype=jnp.int32)
    slot_rows = jnp.sum(jnp.where(slot_hits, row_numbers[None, :, None], 0), axis=1)
    slot_valid = slot_ranks[None, :] < live_count[:, None]
    return (slot_rows, slot_valid)


def global_scaling(block_max, block_sum, block_value, slot_rows, slot_valid, all_rows, head_ids):
    kv_heads, capacity, group_size = block_max.shape
    valid_wide = slot_valid[:, :, None]
    max_table = jnp.full((all_rows, kv_heads, group_size), lowest_value, jnp.float32)
    max_table = max_table.at[slot_rows, head_ids[:, None]].max(
        jnp.where(valid_wide, block_max, lowest_value)
    )
    row_top = lax.pmax(max_table.astype(jnp.bfloat16), ("ctx", "mp")).astype(max_table.dtype)
    factor = jnp.where(valid_wide, jnp.exp(block_max - row_top[slot_rows, head_ids[:, None]]), 0.0)
    return (block_value * factor[..., None], block_sum * factor)


def per_device(
    query,
    keys,
    values,
    chosen,
    residual,
    output_weight,
    norm_gain,
    gate_weight,
    up_weight,
    down_weight,
):
    kv_heads = query.shape[1]
    group_size = query.shape[2]
    head_dim = query.shape[3]
    score_scale = head_dim ** (-0.5)
    mp_count = lax.axis_size("mp")
    ctx_place = lax.axis_index("ctx")
    mp_place = lax.axis_index("mp")
    own_part = ctx_place * mp_count + mp_place
    all_queries = lax.all_gather(query, ("ctx", "mp"), axis=0, tiled=True)
    all_rows = all_queries.shape[0]
    capacity = min(4 * ROW_DEV * KEPT_PARTITIONS, all_rows)
    slot_rows, slot_valid = find_slots(chosen, own_part, capacity)
    head_ids = jnp.arange(kv_heads, dtype=jnp.int32)
    picked = all_queries[slot_rows, head_ids[:, None]].reshape(
        kv_heads, capacity * group_size, head_dim
    )

    def attend(inputs):
        query_block, key_block, value_block = inputs
        scores = (
            lax.dot_general(
                query_block, key_block, (((1,), (1,)), ((), ())), preferred_element_type=jnp.float32
            )
            * score_scale
        )
        block_max = jnp.max(scores, axis=1)
        probs = jnp.exp(scores - block_max[:, None])
        block_sum = jnp.sum(probs, axis=1)
        block_value = jnp.dot(
            probs.astype(jnp.bfloat16), value_block, preferred_element_type=jnp.float32
        )
        return (block_max, block_sum, block_value)

    block_max, block_sum, block_value = lax.map(attend, (picked, keys[0], values[0]))
    block_max = block_max.reshape(kv_heads, capacity, group_size)
    block_sum = block_sum.reshape(kv_heads, capacity, group_size)
    block_value = block_value.reshape(kv_heads, capacity, group_size, head_dim)
    weighted, scaled_sum = global_scaling(
        block_max, block_sum, block_value, slot_rows, slot_valid, all_rows, head_ids
    )
    numerator = jnp.zeros((all_rows, kv_heads, group_size, head_dim), jnp.float32)
    numerator = numerator.at[slot_rows, head_ids[:, None]].add(weighted).reshape(all_rows, -1)
    denominator = jnp.zeros((all_rows, kv_heads, group_size), jnp.float32)
    denominator = denominator.at[slot_rows, head_ids[:, None]].add(scaled_sum).reshape(all_rows, -1)
    numerator, denominator = (
        lax.psum_scatter(numerator, "ctx", scatter_dimension=1, tiled=True),
        lax.psum_scatter(denominator, "ctx", scatter_dimension=1, tiled=True),
    )
    numerator, denominator = (
        lax.psum(numerator.astype(jnp.bfloat16), "mp").astype(jnp.float32),
        lax.psum(denominator.astype(jnp.bfloat16), "mp").astype(jnp.float32),
    )
    attended = (
        (numerator.reshape(all_rows, -1, head_dim) / denominator[:, :, None])
        .reshape(all_rows, -1)
        .astype(jnp.bfloat16)
    )
    rows_here = attended
    projected = lax.psum_scatter(
        jnp.dot(rows_here, output_weight, preferred_element_type=jnp.float32),
        "ctx",
        scatter_dimension=0,
        tiled=True,
    )
    stream = (residual.astype(jnp.float32) + projected).astype(jnp.bfloat16)
    stream_wide = stream.astype(jnp.float32)
    squares = lax.psum(jnp.sum(stream_wide * stream_wide, axis=1), "mp")
    normed = (
        stream_wide * lax.rsqrt(squares / MODEL_WIDTH + norm_eps)[:, None] * norm_gain
    ).astype(jnp.bfloat16)
    row_piece = lax.all_gather(normed, "ctx", axis=0, tiled=True)
    gate_piece = jnp.dot(row_piece, gate_weight, preferred_element_type=jnp.float32)
    up_piece = jnp.dot(row_piece, up_weight, preferred_element_type=jnp.float32)
    gate_up = jnp.stack([gate_piece, up_piece], axis=1)
    gate_up = lax.psum(gate_up.astype(jnp.bfloat16), "mp").astype(jnp.float32)
    hidden = (jax.nn.silu(gate_up[:, 0]) * gate_up[:, 1]).astype(jnp.bfloat16)
    rows_here = hidden
    update = lax.psum_scatter(
        jnp.dot(rows_here, down_weight, preferred_element_type=jnp.float32),
        "ctx",
        scatter_dimension=0,
        tiled=True,
    ).astype(jnp.bfloat16)
    return (stream, update)


def solution(mesh):
    return jax.shard_map(
        per_device,
        mesh=mesh,
        in_specs=(
            P(("ctx", "mp"), None, None, None),
            P(("ctx", "mp"), None, None, None),
            P(("ctx", "mp"), None, None, None),
            P(),
            P("ctx", "mp"),
            P("ctx", "mp"),
            P("mp"),
            P("mp", "ctx"),
            P("mp", "ctx"),
            P("ctx", "mp"),
        ),
        out_specs=(P("ctx", "mp"), P("ctx", "mp")),
        check_vma=False,
    )
```

profile of v0, /device:TPU:1, one launch (start us, length us, event | category | flops | bytes accessed | tf_op | source)
XLA Modules:
  0.0 1395.4 jit_solution(8512046623604453106)
XLA Ops:
  10.5 120.7 %all-gather.4.cloned.1.call-done = bf16[256,8,8,128]{3,2,1,0:T(8,128)(2,1)} async-done(((bf16[1,8,8,128]{3,2,1,0:T(8,128)(2,1)}), bf16[256,8,8,128]{3,2,1,0:T(8,128)(2,1)}) %all-gather.4.cloned.1.call-update) | async-done | bytes 4194320 | tf_op jit(solution)/shard_map/all_gather | solution.py:59
  131.1 4.5 gather_fusion
  135.7 43.1 %while.14 = (s32[]{:T(128)}, f32[8,512]{1,0:T(8,128)S(1)}, f32[8,512]{1,0:T(8,128)S(1)}, f32[8,512,128]{2,1,0:T(8,128)}, bf16[8,512,128]{2,1,0:T(8,128)(2,1)S(1)...) while((s32[]{:T(128)}, f32[8,512]{1,0:T(8,128)S(1)}, ...), condition=%wide.region_7.8_spmd, body=%wide.region_4.7_spmd.sunk | while | flops 545258496 | bytes 14043245 | solution.py:84
  135.7 1.8 multiply_reduce_fusion.2
  138.4 2.6 fusion.58
  141.1 1.8 multiply_reduce_fusion.2
  143.7 2.6 fusion.58
  146.4 1.8 multiply_reduce_fusion.2
  149.1 2.6 fusion.58
  154.5 2.6 fusion.58
  157.2 1.8 multiply_reduce_fusion.2
  159.9 2.6 fusion.58
  165.3 2.6 fusion.58
  170.6 2.6 fusion.58
  176.0 2.6 fusion.58
  179.1 24.1 %scatter_fusion = f32[256,8,8]{2,1,0:T(8,128)S(1)} fusion(f32[256,8,8]{2,1,0:T(8,128)S(1)} %broadcast_in_dim.58, s32[512]{0:T(512)S(1)} %reshape.128, f32[512,8]{1,0:T(8,128)S(1)} %bitcast.93), kind=kCustom, calls=%fused_computation.2 | custom fusion | flops 4096 | bytes 53248 | tf_op jit(solution)/shard_map/scatter-max | solution.py:31
  203.3 78.0 %pmax.7 = bf16[256,8,8]{2,1,0:T(8,128)(2,1)S(1)} all-reduce(bf16[256,8,8]{2,1,0:T(8,128)(2,1)S(1)} %convert_element_type.58), channel_id=1, replica_groups=mesh['ctx'=64,'mp'=4] {'ctx','mp'}, use_global_device_ids=true, to_apply=%region_10.11 | all-reduce | flops 16384 | bytes 65536 | tf_op jit(solution)/shard_map/pmax | solution.py:34
  281.6 2.6 gather_fusion.1
  284.4 2.3 bitcast_multiply_fusion
  286.7 4.3 broadcast_in_dim.52
  290.9 63.9 %scatter_fusion.1 = f32[256,8,8,128]{3,2,1,0:T(8,128)} fusion(f32[256,8,8,128]{3,2,1,0:T(8,128)} %broadcast_in_dim.52, s32[512]{0:T(512)S(1)} %reshape.128, f32[512,8,128]{2,1,0:T(8,128)S(1)} %bitcast.89), kind=kCustom, calls=%fused_computation.3 | custom fusion | flops 524288 | bytes 6295552 | tf_op jit(solution)/shard_map/scatter-add | solution.py:92
  354.8 14.3 %copy.18 = f32[32,8,64,128]{3,1,2,0:T(8,128)} copy(f32[32,8,64,128]{3,2,1,0:T(8,128)} %bitcast.87) | data formatting | bytes 16777216
  369.2 144.7 %reduce-scatter.2.cloned.1.call-done = f32[256,128]{1,0:T(8,128)} async-done(((f32[256,8192]{1,0:T(8,128)}), f32[256,128]{1,0:T(8,128)}) %reduce-scatter.2.cloned.1.call-update) | async-done | bytes 131088 | tf_op jit(solution)/shard_map/reduce_scatter | solution.py:96
  516.4 24.1 %scatter_fusion.2 = f32[256,8,8]{2,1,0:T(8,128)S(1)} fusion(f32[256,8,8]{2,1,0:T(8,128)S(1)} %broadcast_in_dim.61, s32[512]{0:T(512)S(1)} %reshape.128, f32[512,8]{1,0:T(8,128)S(1)} %bitcast.94), kind=kCustom, calls=%fused_computation.4 | custom fusion | flops 4096 | bytes 53248 | tf_op jit(solution)/shard_map/scatter-add | solution.py:94
  540.9 246.5 %all-reduce = bf16[256,64]{0,1:T(8,128)(2,1)S(1)} all-reduce(f32[256,64]{0,1:T(8,128)S(1)} %bitcast.97), channel_id=3, replica_groups=mesh['ctx'=64,'mp'=4] {'ctx'}, use_global_device_ids=true, to_apply=%region_15.16.clone | all-reduce | flops 16384 | bytes 98304
  788.1 7.6 psum.29
  795.7 2.9 fusion.30
  799.4 185.7 %all-reduce.12.cloned.1.call-done = f32[256,2048]{1,0:T(8,128)} async-done(((f32[256,2048]{1,0:T(8,128)}), f32[256,2048]{1,0:T(8,128)}) %all-reduce.12.cloned.1.call-update) | async-done | bytes 2097168
  986.0 8.4 psum.30
  995.2 77.2 %all-gather.6.cloned.1.call-done = bf16[64,4,2048]{2,1,0:T(4,128)(2,1)} async-done(((bf16[1,4,2048]{2,1,0:T(4,128)(2,1)}), bf16[64,4,2048]{2,1,0:T(4,128)(2,1)}) %all-gather.6.cloned.1.call-update) | async-done | bytes 1048592 | tf_op jit(solution)/shard_map/all_gather | solution.py:121
  1076.7 41.9 %all-reduce.10.cloned.1.call-done = bf16[256,2,224]{0,2,1:T(8,128)(2,1)} async-done(((bf16[256,2,224]{0,2,1:T(8,128)(2,1)}), bf16[256,2,224]{0,2,1:T(8,128)(2,1)}) %all-reduce.10.cloned.1.call-update) | async-done | bytes 229392 | tf_op jit(solution)/shard_map/psum | solution.py:125
  1120.1 267.1 %all-reduce.13 = bf16[256,2048]{1,0:T(8,128)(2,1)} all-reduce(f32[256,2048]{1,0:T(8,128)S(1)} %fusion.27), channel_id=5, replica_groups=mesh['ctx'=64,'mp'=4] {'ctx'}, use_global_device_ids=true, to_apply=%region_21.22.clone | all-reduce | flops 524288 | bytes 3145728
  (92 shorter events, 31.1 us)
Async XLA Ops:
  7.2 1112.5 %copy-start = (bf16[224,2048]{1,0:T(8,128)(2,1)S(1)}, bf16[224,2048]{1,0:T(8,128)(2,1)}, u32[]{:S(2)}) copy-start(bf16[224,2048]{1,0:T(8,128)(2,1)} %param.21) | copy-start | bytes 2752516
  7.2 124.0 %all-gather.4.cloned.1.call-start = ((), (), s32[]{:S(2)}) async-start(), calls=%async_computation.1 | async-start | bytes 4210688 | tf_op jit(solution)/shard_map/all_gather | solution.py:59
  7.9 506.0 %reduce-scatter.2.cloned.1.call-start = ((), (), s32[]{:S(2)}) async-start(), calls=%async_computation.2 | async-start | bytes 8519680 | tf_op jit(solution)/shard_map/reduce_scatter | solution.py:96
  369.1 146.6 %copy-start.5 = (u32[256]{0:T(256)S(1)}, u32[256]{0:T(256)}, u32[]{:S(2)}) copy-start(u32[256]{0:T(256)} %constant.148) | copy-start | bytes 3076
  369.1 426.6 %all-reduce.8.cloned.1.call-start = ((), (), s32[]{:S(2)}) async-start(), calls=%async_computation.3 | async-start | bytes 131072 | tf_op jit(solution)/shard_map/psum | solution.py:100
  515.5 469.6 %all-reduce.12.cloned.1.call-start = ((), (), s32[]{:S(2)}) async-start(), calls=%async_computation.6 | async-start | bytes 4194304
  516.4 468.6 %copy-start.3 = (bf16[4,2048]{1,0:T(4,128)(2,1)S(1)}, bf16[4,2048]{1,0:T(4,128)(2,1)}, u32[]{:S(2)}) copy-start(bf16[4,2048]{1,0:T(4,128)(2,1)} %param.16) | copy-start | bytes 49156
  540.6 453.9 %copy-start.4 = (f32[2048]{0:T(1024)S(1)}, f32[2048]{0:T(1024)}, u32[]{:S(2)}) copy-start(f32[2048]{0:T(1024)} %param.18) | copy-start | bytes 24580
  540.6 533.2 %copy-start.1 = (bf16[2048,224]{0,1:T(8,128)(2,1)S(1)}, bf16[2048,224]{0,1:T(8,128)(2,1)}, u32[]{:S(2)}) copy-start(bf16[2048,224]{0,1:T(8,128)(2,1)} %param.20) | copy-start | bytes 2752516
  798.7 273.7 %all-gather.6.cloned.1.call-start = ((), (), s32[]{:S(2)}) async-start(), calls=%async_computation.5 | async-start | bytes 1064960 | tf_op jit(solution)/shard_map/all_gather | solution.py:121
  986.0 134.1 %copy-start.2 = (bf16[4,2048]{1,0:T(4,128)(2,1)}, bf16[4,2048]{1,0:T(4,128)(2,1)S(1)}, u32[]{:S(2)}) copy-start(bf16[4,2048]{1,0:T(4,128)(2,1)S(1)} %get-tuple-element.59) | copy-start | bytes 49156
  995.2 123.5 %all-reduce.10.cloned.1.call-start = ((), (), s32[]{:S(2)}) async-start(), calls=%async_computation.4 | async-start | bytes 458752 | tf_op jit(solution)/shard_map/psum | solution.py:125
Sparse Core Ops, SparseCore 0:
  11.7 119.3 all-gather.3
  369.2 144.6 reduce-scatter.1
  516.3 47.1 all-reduce.7
  798.8 186.2 all-reduce.11
  995.3 77.0 all-gather.5
  1076.8 41.7 all-reduce.9
where the time goes:
time: 1400 us
  blocking collectives  608 us (43%)
  waiting for transfers between devices  571 us (41%)
  other arithmetic  128 us (9%)
  matrix products  41.1 us (3%)
  local copies, waits for them, and re-layouts  31.6 us (2%)
  between operations  15 us (1%)
    unnamed x2, blocking collectives  514 us
    unnamed x7, waiting for transfers between devices  186 us
    reduce_scatter x1, waiting for transfers between devices, per_device(): lax.psum_scatter(numerator, 'ctx', scatter_dimension=1, tiled=True)  145 us
    all_gather x1, waiting for transfers between devices, per_device(): all_queries = lax.all_gather(query, ('ctx', 'mp'), axis=0, tiled=True)  121 us
    pmax x1, blocking collectives, global_scaling(): lax.pmax(max_table.astype(jnp.bfloat16), ('ctx', 'mp'))  78 us
    all_gather x1, waiting for transfers between devices, per_device(): row_piece = lax.all_gather(normed, 'ctx', axis=0, tiled=True)  77.2 us
    scatter-add x1, other arithmetic, per_device(): numerator.at[slot_rows, head_ids[:, None]].add(weighted)  63.9 us
    psum x1, waiting for transfers between devices, per_device(): gate_up = lax.psum(gate_up.astype(jnp.bfloat16), 'mp').astype(jnp.float32)  41.9 us
  transfers between devices with their start and end apart: 6, of which 5 were waited for; matrix products, arithmetic and copies ran while one was open for 2% of the time, Pallas kernels for 0%

commit v1 on v0

v1 whole, which is shorter than its diff:
```python
import functools
import math

import jax
import jax.numpy as jnp
from jax import lax
from jax.experimental import pallas as pl
from jax.experimental.pallas import tpu as pltpu
from jax.sharding import PartitionSpec as P

NX, NY, NZ, NK = 4, 4, 8, 2
CTX = NY * NZ * NK
ROWS, HEADS, GROUP, WIDTH = 256, 8, 8, 128
KEYS, SLOTS = 2048, 64
MODEL, LOCAL, UNITS = 8192, 2048, 224
MSG = SLOTS + 16
EPS = 1e-5
LOWEST = -1e30
SCALE = WIDTH**-0.5 * math.log2(math.e)
MESH = pl.DeviceIdType.MESH
VMEM_LIMIT = 56 * 1024 * 1024
F32, BF16 = jnp.float32, jnp.bfloat16


def place():
    c = lax.axis_index("ctx")
    x = lax.axis_index("mp")
    return c, x, c // (NZ * NK), (c // NK) % NZ, c % NK


def ctx_of(y, z, k):
    return (y * NZ + z) * NK + k


def remote(src, dst, send_sem, recv_sem, ctx, mp):
    return pltpu.make_async_remote_copy(
        src_ref=src,
        dst_ref=dst,
        send_sem=send_sem,
        recv_sem=recv_sem,
        device_id=(ctx, mp),
        device_id_type=MESH,
    )


def dot(a, b, da, db):
    return lax.dot_general(a, b, (((da,), (db,)), ((), ())), preferred_element_type=F32)


def attend_kernel(
    slots_ref, own_ref, rank_ref, keys_ref, values_ref, out_ref,
    qbuf, kbuf, vbuf, q32, o32, st32, sendbuf,
    k_sem, v_sem,
    z_send, z_recv, p2_send, p2_recv, p3_send, p3_recv, c_send, c_recv,
    a_send, a_recv,
):
    c, x, y, z, k = place()

    barrier = pltpu.get_barrier_semaphore()

    def greet(j, carry):
        @pl.when(j != c)
        def _():
            pl.semaphore_signal(barrier, inc=1, device_id=(j, x), device_id_type=MESH)

        return carry

    lax.fori_loop(0, CTX, greet, 0)
    for j in range(1, NX):
        pl.semaphore_signal(barrier, inc=1, device_id=(c, (x + j) % NX), device_id_type=MESH)

    def load(t, carry):
        h = (c // GROUP + t) % HEADS
        pltpu.make_async_copy(keys_ref.at[h], kbuf.at[h], k_sem.at[h]).start()
        pltpu.make_async_copy(values_ref.at[h], vbuf.at[h], v_sem.at[h]).start()
        return carry

    lax.fori_loop(0, HEADS, load, 0)

    row_a = ((k * NX + x) * NY + y) * NZ
    row_b = ((k * NY + y) * NX + x) * NZ
    qbuf[0:2, row_a + z] = own_ref[0:2]
    qbuf[2:4, row_b + z] = own_ref[2:4]
    pl.semaphore_wait(barrier, CTX - 1 + NX - 1)

    z_copies = []
    for j in range(1, NZ):
        to = ctx_of(y, (z + j) % NZ, k)
        for half, row in ((0, row_a), (1, row_b)):
            ref = qbuf.at[pl.ds(2 * half, 2), row + z]
            cp = remote(ref, ref, z_send.at[half, j - 1], z_recv.at[half, j - 1], to, x)
            cp.start()
            z_copies.append(cp)
    for cp in z_copies:
        cp.wait_recv()

    p2 = []
    for j in range(1, 4):
        ref = qbuf.at[0:2, pl.ds(row_a, NZ)]
        cp = remote(ref, ref, p2_send.at[0, j - 1], p2_recv.at[0, j - 1], ctx_of((y + j) % NY, z, k), x)
        cp.start()
        p2.append(cp)
        ref = qbuf.at[2:4, pl.ds(row_b, NZ)]
        cp = remote(ref, ref, p2_send.at[1, j - 1], p2_recv.at[1, j - 1], c, (x + j) % NX)
        cp.start()
        p2.append(cp)
    for cp in p2:
        cp.wait_recv()

    other = ctx_of(y, z, 1 - k)
    base = {0: k * NX + x, 1: k * NY + y}
    order = (0, 2, 1, 3)
    p3 = {}
    cores = []

    def pass_on(hp, block, n):
        ref = qbuf.at[hp, pl.ds(block * 32, 32)]
        cp = remote(ref, ref, c_send.at[hp, n], c_recv.at[hp, n], other, x)
        cp.start()
        cores.append(cp)

    for hp in order:
        for j in range(1, 4):
            ref = qbuf.at[hp, pl.ds(base[hp // 2] * 32, 32)]
            if hp < 2:
                cp = remote(ref, ref, p3_send.at[hp, j - 1], p3_recv.at[hp, j - 1], c, (x + j) % NX)
            else:
                cp = remote(ref, ref, p3_send.at[hp, j - 1], p3_recv.at[hp, j - 1], ctx_of((y + j) % NY, z, k), x)
            cp.start()
            p3[hp, j] = cp
    for hp in order:
        pass_on(hp, base[hp // 2], 0)
    for hp in order:
        for j in range(1, 4):
            p3[hp, j].wait_recv()
            source = (x - j + NX) % NX if hp < 2 else (y - j + NY) % NY
            pass_on(hp, k * 4 + source, j)
    for cp in cores:
        cp.wait_recv()

    slot_iota = lax.broadcasted_iota(jnp.int32, (SLOTS, ROWS), 0).astype(F32)

    def head(t, carry):
        h = (c // GROUP + t) % HEADS
        hp = h // 2
        upper = (h % 2) == 1
        pltpu.make_async_copy(keys_ref.at[h], kbuf.at[h], k_sem.at[h]).wait()
        pltpu.make_async_copy(values_ref.at[h], vbuf.at[h], v_sem.at[h]).wait()

        def pick(i, carry2):
            for u in range(8):
                s = i * 8 + u
                tile = qbuf[hp, slots_ref[h * SLOTS + s]].astype(F32)
                q32[pl.ds(pl.multiple_of(s * 8, 8), 8), :] = jnp.where(upper, tile[8:16], tile[0:8])
            return carry2

        lax.fori_loop(0, SLOTS // 8, pick, 0)

        for b in range(2):
            at = pl.ds(b * 256, 256)
            s = dot(q32[at, :].astype(BF16), kbuf[h], 1, 1)
            top = (jnp.max(s, axis=1, keepdims=True) * SCALE).astype(BF16).astype(F32)
            p = jnp.exp2(s * SCALE - top)
            total = jnp.sum(p, axis=1, keepdims=True)
            o32[at, :] = dot(p.astype(BF16), vbuf[h], 1, 0)
            lane = lax.broadcasted_iota(jnp.int32, (256, WIDTH), 1)
            st32[at, :] = jnp.where(lane == 0, top, total)

        hit = slot_iota == rank_ref[pl.ds(h, 1), :]
        for g in range(GROUP):
            n = h * GROUP + g
            sendbuf[n, 0:SLOTS, :] = o32[pl.ds(g, SLOTS, stride=GROUP), :].astype(BF16)
            st = st32[pl.ds(g, SLOTS, stride=GROUP), :]
            top = jnp.sum(jnp.where(hit, st[:, 0:1], 0.0), axis=0, keepdims=True)
            total = jnp.sum(jnp.where(hit, st[:, 1:2], 0.0), axis=0, keepdims=True)
            high = total.astype(BF16).astype(F32)
            low = total - high
            tile = jnp.concatenate(
                [
                    top[:, :128], top[:, 128:], high[:, :128], high[:, 128:],
                    low[:, :128], low[:, 128:], jnp.zeros((10, 128), F32),
                ],
                axis=0,
            )
            sendbuf[n, SLOTS:MSG, :] = tile.astype(BF16)

            @pl.when(n != c)
            def _():
                remote(sendbuf.at[n], out_ref.at[c], a_send.at[n], a_recv.at[c], n, x).start()

            @pl.when(n == c)
            def _():
                out_ref[c] = sendbuf[n]

        return carry

    lax.fori_loop(0, HEADS, head, 0)

    for cp in z_copies:
        cp.wait_send()
    for cp in p2:
        cp.wait_send()
    for cp in p3.values():
        cp.wait_send()
    for cp in cores:
        cp.wait_send()

    def finish(j, carry):
        @pl.when(j != c)
        def _():
            cp = remote(sendbuf.at[j], out_ref.at[j], a_send.at[j], a_recv.at[j], j, x)
            cp.wait_recv()
            cp.wait_send()

        return carry

    lax.fori_loop(0, CTX, finish, 0)


def swap4(v):
    return pltpu.roll(v, 4, 1)


def regroup(acc, out_ref):
    parts = [acc[:, b * 512 : (b + 1) * 512].reshape(4, 8, 512) for b in range(4)]
    lower = lax.broadcasted_iota(jnp.int32, (4, 8, 512), 1) < 4
    even = [jnp.where(lower, parts[b], swap4(parts[b + 1])) for b in (0, 2)]
    odd = [jnp.where(lower, swap4(parts[b]), parts[b + 1]) for b in (0, 2)]
    for t in range(4):
        out_ref[2 * t] = jnp.concatenate([even[0][t], even[1][t]], axis=0).astype(BF16)
        out_ref[2 * t + 1] = jnp.concatenate([odd[0][t], odd[1][t]], axis=0).astype(BF16)


def ungroup(src_ref, store):
    a = src_ref[...].astype(F32)
    lower = lax.broadcasted_iota(jnp.int32, (8, 512), 0) < 4
    columns = [[], [], [], []]
    for t in range(4):
        for q in range(2):
            e = a[2 * t, 8 * q : 8 * q + 8]
            o = a[2 * t + 1, 8 * q : 8 * q + 8]
            columns[2 * q].append(jnp.where(lower, e, pltpu.roll(o, 4, 0)))
            columns[2 * q + 1].append(jnp.where(lower, pltpu.roll(e, 4, 0), o))
    for b in range(4):
        store(b, jnp.concatenate(columns[b], axis=0).astype(BF16))


def layer_kernel(
    msg_ref, rank_ref, residual_ref, gain_ref, wo_hbm, wg_hbm, wu_hbm, wd_hbm,
    stream_ref, update_ref,
    wo, wg, wu, wd, weight, stats, weights, num_t, xmsg, att_t,
    core_out, core_in, y_out, y_in, z_out, z_in,
    z_all, x_all, gu32, gu_out, gu_in, hid,
    w_sem, x_send, x_recv,
    c_send, c_recv, y_send, y_recv, z_send, z_recv,
    gz_send, gz_recv, gy_send, gy_recv, gc_send, gc_recv,
    r_send, r_recv, h_send, h_recv,
):
    c, x, y, z, k = place()
    other = ctx_of(y, z, 1 - k)
    barrier = pltpu.get_barrier_semaphore()
    pl.semaphore_signal(barrier, inc=1, device_id=(other, x), device_id_type=MESH)
    for j in range(1, NX):
        pl.semaphore_signal(barrier, inc=1, device_id=(c, (x + j) % NX), device_id_type=MESH)
    for j in range(1, NY):
        pl.semaphore_signal(barrier, inc=1, device_id=(ctx_of((y + j) % NY, z, k), x), device_id_type=MESH)
    for j in range(1, NZ):
        pl.semaphore_signal(barrier, inc=1, device_id=(ctx_of(y, (z + j) % NZ, k), x), device_id_type=MESH)

    loads = [
        pltpu.make_async_copy(wo_hbm, wo, w_sem.at[0]),
        pltpu.make_async_copy(wg_hbm, wg, w_sem.at[1]),
        pltpu.make_async_copy(wu_hbm, wu, w_sem.at[2]),
        pltpu.make_async_copy(wd_hbm, wd.at[pl.ds(0, UNITS)], w_sem.at[3]),
    ]
    for cp in loads:
        cp.start()
    wd[UNITS:256, :] = jnp.zeros((256 - UNITS, LOCAL), BF16)

    def spread(s, carry):
        stats[pl.ds(pl.multiple_of(s * 16, 16), 16), :] = msg_ref[s, SLOTS:MSG, :].astype(F32)
        return carry

    lax.fori_loop(0, CTX, spread, 0)

    def row_of(n):
        return jnp.concatenate([stats[pl.ds(2 * n + i, CTX, stride=16), :] for i in range(2)], axis=1)

    listed = rank_ref[...] >= 0.0
    top_each = jnp.where(listed, row_of(0), LOWEST)
    top = jnp.max(top_each, axis=0, keepdims=True)
    w = jnp.where(listed, jnp.exp2(top_each - top), 0.0).astype(BF16).astype(F32)
    weights[...] = w
    den = jnp.sum(w * (row_of(1) + row_of(2)), axis=0, keepdims=True)

    num_t[...] = jnp.zeros_like(num_t)
    slot_iota = lax.broadcasted_iota(jnp.int32, (SLOTS, ROWS), 0).astype(F32)

    def merge(i, carry):
        for u in range(4):
            s = i * 4 + u
            hit = slot_iota == rank_ref[pl.ds(s, 1), :]
            weight[pl.ds(u * SLOTS, SLOTS), :] = jnp.where(hit, weights[pl.ds(s, 1), :], 0.0).astype(BF16)
        values = jnp.concatenate([msg_ref[i * 4 + u, 0:SLOTS, :] for u in range(4)], axis=0)
        num_t[...] += dot(values, weight[...], 0, 0)
        return carry

    lax.fori_loop(0, CTX // 4, merge, 0)

    xmsg[x, 0:WIDTH, :] = num_t[...].astype(BF16)
    den_high = den.astype(BF16).astype(F32)
    xmsg[x, WIDTH : WIDTH + 16, :] = jnp.concatenate(
        [top, den_high, den - den_high, jnp.zeros((13, ROWS), F32)], axis=0
    ).astype(BF16)
    pl.semaphore_wait(barrier, 1 + NX - 1 + NY - 1 + NZ - 1)
    copies = []
    for j in range(1, NX):
        cp = remote(xmsg.at[x], xmsg.at[x], x_send.at[j - 1], x_recv.at[j - 1], c, (x + j) % NX)
        cp.start()
        copies.append(cp)
    for cp in copies:
        cp.wait()
    tails = [xmsg[i, WIDTH : WIDTH + 16, :].astype(F32) for i in range(NX)]
    best = functools.reduce(jnp.maximum, [v[0:1] for v in tails])
    num, den = 0.0, 0.0
    for i in range(NX):
        f = jnp.exp2(tails[i][0:1] - best)
        den = den + f * (tails[i][1:2] + tails[i][2:3])
        num = num + f * xmsg[i, 0:WIDTH, :].astype(F32)
    att_t[...] = (num / den).astype(BF16)

    def half(v_ref, which):
        return v_ref[:, pl.ds(pl.multiple_of(which * 128, 128), 128)]

    def reduce_scatter(n, piece):
        core_out[n] = piece(1 - k).astype(BF16)
        cp = remote(core_out.at[n], core_in.at[n], c_send.at[n], c_recv.at[n], other, x)
        cp.start()
        mine = piece(k)
        cp.wait_recv()
        total = mine + core_in[n].astype(F32)
        y_out[n] = total.reshape(NY, 32, LOCAL).astype(BF16)
        pending = [cp]
        arrivals = []
        for j in range(1, NY):
            to = (y + j) % NY
            cp = remote(y_out.at[n, to], y_in.at[n, j - 1], y_send.at[n, j - 1], y_recv.at[n, j - 1], ctx_of(to, z, k), x)
            cp.start()
            pending.append(cp)
            arrivals.append(cp)
        acc = y_out[n, y].astype(F32)
        for j, cp in enumerate(arrivals):
            cp.wait_recv()
            acc = acc + y_in[n, j].astype(F32)
        regroup(acc, z_out.at[n])
        arrivals = []
        for j in range(1, NZ):
            to = (z + j) % NZ
            cp = remote(z_out.at[n, to], z_in.at[n, j - 1], z_send.at[n, j - 1], z_recv.at[n, j - 1], ctx_of(y, to, k), x)
            cp.start()
            pending.append(cp)
            arrivals.append(cp)
        acc = z_out[n, z].astype(F32)
        for j, cp in enumerate(arrivals):
            cp.wait_recv()
            acc = acc + z_in[n, j].astype(F32)
        return acc, pending

    loads[0].wait()
    projected, pending = reduce_scatter(0, lambda which: dot(half(att_t, which), wo[...], 0, 0))
    stream = (residual_ref[...].astype(F32) + projected).astype(BF16)
    stream_ref[...] = stream

    z_all[z] = stream
    arrivals = []
    for j in range(1, NZ):
        cp = remote(z_all.at[z], z_all.at[z], gz_send.at[j - 1], gz_recv.at[j - 1], ctx_of(y, (z + j) % NZ, k), x)
        cp.start()
        pending.append(cp)
        arrivals.append(cp)
    for cp in arrivals:
        cp.wait_recv()

    def put(b, v):
        x_all[k, y, :, b * 512 : (b + 1) * 512] = v

    ungroup(z_all, put)
    arrivals = []
    for j in range(1, NY):
        cp = remote(x_all.at[k, y], x_all.at[k, y], gy_send.at[j - 1], gy_recv.at[j - 1], ctx_of((y + j) % NY, z, k), x)
        cp.start()
        pending.append(cp)
        arrivals.append(cp)
    for cp in arrivals:
        cp.wait_recv()
    core_copy = remote(x_all.at[k], x_all.at[k], gc_send, gc_recv, other, x)
    core_copy.start()
    pending.append(core_copy)
    loads[1].wait()
    loads[2].wait()

    def gate_up(which):
        rows = x_all[which].reshape(128, LOCAL)
        wide = rows.astype(F32)
        squares = jnp.sum(wide * wide, axis=1, keepdims=True)
        scaled = (wide * gain_ref[...]).astype(BF16)
        for n, weight_ref in enumerate((wg, wu)):
            gu32[n, which, :, 0:UNITS] = dot(scaled, weight_ref[...], 1, 0).astype(BF16)
        high = squares.astype(BF16).astype(F32)
        lane = lax.broadcasted_iota(jnp.int32, (128, 256 - UNITS), 1)
        gu32[0, which, :, UNITS:256] = jnp.where(lane == 0, high, squares - high).astype(BF16)
        gu32[1, which, :, UNITS:256] = jnp.zeros((128, 256 - UNITS), BF16)

    gate_up(k)
    core_copy.wait_recv()
    gate_up(1 - k)

    for q in range(NX):
        for n in range(2):
            gu_out[q, n] = gu32[n, q // 2, (q % 2) * 64 : (q % 2) * 64 + 64, :]
    arrivals = []
    for j in range(1, NX):
        to = (x + j) % NX
        cp = remote(gu_out.at[to], gu_in.at[j - 1], r_send.at[j - 1], r_recv.at[j - 1], c, to)
        cp.start()
        pending.append(cp)
        arrivals.append(cp)
    acc = gu_out[x].astype(F32)
    for j, cp in enumerate(arrivals):
        cp.wait_recv()
        acc = acc + gu_in[j].astype(F32)
    squares = acc[0, :, UNITS : UNITS + 1] + acc[0, :, UNITS + 1 : UNITS + 2]
    factor = lax.rsqrt(squares / MODEL + EPS)
    gate = acc[0] * factor
    up = acc[1] * factor
    lane = lax.broadcasted_iota(jnp.int32, (64, 256), 1)
    hidden = jnp.where(lane < UNITS, gate / (1.0 + jnp.exp(-gate)) * up, 0.0)
    hid[x] = hidden.astype(BF16)
    arrivals = []
    for j in range(1, NX):
        cp = remote(hid.at[x], hid.at[x], h_send.at[j - 1], h_recv.at[j - 1], c, (x + j) % NX)
        cp.start()
        pending.append(cp)
        arrivals.append(cp)
    for cp in arrivals:
        cp.wait_recv()
    loads[3].wait()

    def down(which):
        rows = hid[pl.ds(which * 2, 2)].reshape(128, 256)
        return dot(rows, wd[...], 1, 0)

    updated, rest = reduce_scatter(1, down)
    update_ref[...] = updated.astype(BF16)
    for cp in pending + rest:
        cp.wait_send()


def prelude(chosen, p, head, mp):
    rows = jnp.arange(ROWS, dtype=jnp.int32)
    k, y, z, m = rows // 128, (rows // 32) % 4, (rows // 4) % 8, rows % 4
    pos_a = ((k * NX + m) * NY + y) * NZ + z
    pos_b = ((k * NY + y) * NX + m) * NZ + z
    ordered = chosen.reshape(HEADS, NY, NZ, NK, 4, 16).transpose(0, 3, 1, 2, 4, 5).reshape(HEADS, ROWS, 16)
    before = (rows[:, None] < rows[None, :]).astype(BF16)

    def ranks(member):
        count = jnp.dot(member.astype(BF16), before, preferred_element_type=F32)
        return jnp.where(member, count, -1.0)

    own = ranks(jnp.any(ordered == p, axis=2))
    spots = jnp.arange(SLOTS, dtype=F32)
    pos = jnp.where(jnp.arange(HEADS)[:, None] < 4, pos_a[None], pos_b[None])
    slots = jnp.sum(jnp.where(own[:, None, :] == spots[None, :, None], pos[:, None, :], 0), axis=2)
    listed = lax.dynamic_index_in_dim(ordered, head, 0, keepdims=False)
    ids = jnp.arange(CTX, dtype=jnp.int32) * NX + mp
    plane = ranks(jnp.any(listed[None] == ids[:, None, None], axis=2))
    return slots.reshape(-1).astype(jnp.int32), own, plane


def dma(*shape):
    return pltpu.SemaphoreType.DMA(shape)


def per_device(query, keys, values, chosen, residual, output_weight, norm_gain, gate_weight, up_weight, down_weight):
    c = lax.axis_index("ctx")
    x = lax.axis_index("mp")
    slots, own, plane = prelude(chosen, c * NX + x, c // GROUP, x)
    vmem = pl.BlockSpec(memory_space=pltpu.VMEM)
    hbm = pl.BlockSpec(memory_space=pl.ANY)
    messages = pl.pallas_call(
        attend_kernel,
        out_shape=jax.ShapeDtypeStruct((CTX, MSG, WIDTH), BF16),
        in_specs=[pl.BlockSpec(memory_space=pltpu.SMEM), vmem, vmem, hbm, hbm],
        out_specs=vmem,
        scratch_shapes=[
            pltpu.VMEM((4, ROWS, 16, WIDTH), BF16),
            pltpu.VMEM((HEADS, KEYS, WIDTH), BF16),
            pltpu.VMEM((HEADS, KEYS, WIDTH), BF16),
            pltpu.VMEM((SLOTS * GROUP, WIDTH), F32),
            pltpu.VMEM((SLOTS * GROUP, WIDTH), F32),
            pltpu.VMEM((SLOTS * GROUP, WIDTH), F32),
            pltpu.VMEM((CTX, MSG, WIDTH), BF16),
            dma(HEADS), dma(HEADS),
            dma(2, 7), dma(2, 7), dma(2, 3), dma(2, 3), dma(4, 3), dma(4, 3), dma(4, 4), dma(4, 4),
            dma(CTX), dma(CTX),
        ],
        compiler_params=pltpu.CompilerParams(collective_id=0, has_side_effects=True, vmem_limit_bytes=VMEM_LIMIT),
        name="attend",
    )(slots, query.reshape(4, 16, WIDTH), own, keys[0], values[0])
    fold = lambda a: a.reshape(4, 4, 512).transpose(1, 0, 2).reshape(16, 512)
    stream, update = pl.pallas_call(
        layer_kernel,
        out_shape=[jax.ShapeDtypeStruct((16, 512), BF16)] * 2,
        in_specs=[vmem, vmem, vmem, vmem, hbm, hbm, hbm, hbm],
        out_specs=[vmem, vmem],
        scratch_shapes=[
            pltpu.VMEM((WIDTH, LOCAL), BF16),
            pltpu.VMEM((LOCAL, UNITS), BF16),
            pltpu.VMEM((LOCAL, UNITS), BF16),
            pltpu.VMEM((256, LOCAL), BF16),
            pltpu.VMEM((4 * SLOTS, ROWS), BF16),
            pltpu.VMEM((CTX * 16, WIDTH), F32),
            pltpu.VMEM((CTX, ROWS), F32),
            pltpu.VMEM((WIDTH, ROWS), F32),
            pltpu.VMEM((NX, WIDTH + 16, ROWS), BF16),
            pltpu.VMEM((WIDTH, ROWS), BF16),
            pltpu.VMEM((2, 128, LOCAL), BF16),
            pltpu.VMEM((2, 128, LOCAL), BF16),
            pltpu.VMEM((2, NY, 32, LOCAL), BF16),
            pltpu.VMEM((2, NY - 1, 32, LOCAL), BF16),
            pltpu.VMEM((2, NZ, 16, 512), BF16),
            pltpu.VMEM((2, NZ - 1, 16, 512), BF16),
            pltpu.VMEM((NZ, 16, 512), BF16),
            pltpu.VMEM((NK, NY, 32, LOCAL), BF16),
            pltpu.VMEM((2, NK, 128, 256), BF16),
            pltpu.VMEM((NX, 2, 64, 256), BF16),
            pltpu.VMEM((NX - 1, 2, 64, 256), BF16),
            pltpu.VMEM((NX, 64, 256), BF16),
            dma(4), dma(3), dma(3),
            dma(2), dma(2), dma(2, 3), dma(2, 3), dma(2, 7), dma(2, 7),
            dma(7), dma(7), dma(3), dma(3), pltpu.SemaphoreType.DMA, pltpu.SemaphoreType.DMA,
            dma(3), dma(3), dma(3), dma(3),
        ],
        compiler_params=pltpu.CompilerParams(collective_id=1, has_side_effects=True, vmem_limit_bytes=VMEM_LIMIT),
        name="layer",
    )(messages, plane, fold(residual), norm_gain.reshape(1, LOCAL), output_weight, gate_weight, up_weight, down_weight)
    unfold = lambda a: a.reshape(4, 4, 512).transpose(1, 0, 2).reshape(4, LOCAL)
    return unfold(stream), unfold(update)


def solution(mesh):
    return jax.shard_map(
        per_device,
        mesh=mesh,
        in_specs=(
            P(("ctx", "mp"), None, None, None),
            P(("ctx", "mp"), None, None, None),
            P(("ctx", "mp"), None, None, None),
            P(),
            P("ctx", "mp"),
            P("ctx", "mp"),
            P("mp"),
            P("mp", "ctx"),
            P("mp", "ctx"),
            P("ctx", "mp"),
        ),
        out_specs=(P("ctx", "mp"), P("ctx", "mp")),
        check_vma=False,
    )
```

time: 1400 us -> 162 us (0.12)
  blocking collectives: 608 us -> 0 us
  waiting for transfers between devices: 571 us -> 0 us
  Pallas kernels: 0 us -> 146 us
  other arithmetic: 128 us -> 5.08 us
  matrix products: 41.1 us -> 0.97 us
  local copies, waits for them, and re-layouts: 31.6 us -> 9.13 us
  between operations: 15 us -> 0.75 us
    unnamed x2 -> x0, blocking collectives: 514 us -> none
    all_gather x2 -> x0, waiting for transfers between devices: 198 us -> none  [the longest x1 121 us: per_device(): all_queries = lax.all_gather(query, ('ctx', 'mp'), axis=0, tiled=True)]
    unnamed x7 -> x0, waiting for transfers between devices: 186 us -> none
    pallas_call x0 -> x2, Pallas kernels: none -> 146 us  [the longest x1 74.1 us: per_device(): pl.pallas_call(attend_kernel, out_shape=jax.ShapeDtypeStruct((CTX, MSG, W...]
    reduce_scatter x1 -> x0, waiting for transfers between devices: 145 us -> none  [per_device(): lax.psum_scatter(numerator, 'ctx', scatter_dimension=1, tiled=True)]
    scatter-add x2 -> x0, other arithmetic: 88 us -> none  [the longest x1 63.9 us: per_device(): numerator.at[slot_rows, head_ids[:, None]].add(weighted)]
    pmax x1 -> x0, blocking collectives: 78 us -> none  [global_scaling(): lax.pmax(max_table.astype(jnp.bfloat16), ('ctx', 'mp'))]
    psum x2 -> x0, waiting for transfers between devices: 41.9 us -> none  [the longest x1 41.9 us: per_device(): gate_up = lax.psum(gate_up.astype(jnp.bfloat16), 'mp').astype(jnp.float32)]
  transfers between devices with their start and end apart: 6 -> 0, of which waited for: 5 -> 0; matrix products, arithmetic and copies ran while one was open for 2% -> 0% of each run, Pallas kernels for 0% -> 0%
where the time goes in v1:
time: 162 us
  Pallas kernels  146 us (90%)
  local copies, waits for them, and re-layouts  9.13 us (6%)
  other arithmetic  5.08 us (3%)
    pallas_call x1, Pallas kernels, per_device(): pl.pallas_call(attend_kernel, out_shape=jax.ShapeDtypeStruct((CTX, MSG, W...  74.1 us
    pallas_call x1, Pallas kernels, per_device(): pl.pallas_call(layer_kernel, out_shape=[jax.ShapeDtypeStruct((16, 512), B...  71.8 us
    reduce_or x1, other arithmetic, prelude(): own = ranks(jnp.any(ordered == p, axis=2))  4.49 us
    unnamed x9, local copies, waits for them, and re-layouts  3.97 us

profile of v1, /device:TPU:1, one launch (start us, length us, event | category | flops | bytes accessed | tf_op | source)
XLA Modules:
  0.0 161.8 jit_solution(18325931051641738930)
XLA Ops:
  0.6 0.0 copy-start.1
  0.6 0.0 copy-start
  0.7 0.1 broadcast_select_fusion
  0.8 1.5 reshape.159.residual_ref
  2.3 1.3 copy.43
  3.6 4.5 %compare_reduce_fusion.1 = pred[8,2,4,8,4]{0,4,1,3,2:T(4,128)(4,1)S(1)} fusion(s32[8,2,4,8,4,16]{5,0,4,1,3,2:T(8,128)S(1)} %bitcast.21, s32[]{:T(128)S(6)} %add.119), kind=kLoop, calls=%fused_computation.3 | loop fusion | flops 63488 | bytes 133124 | tf_op jit(solution)/shard_map/reduce_or | solution.py:471
  8.1 0.1 copy.46
  8.2 0.1 constant_dynamic-slice_fusion
  8.3 0.1 copy.47
  8.4 0.3 compare_reduce_fusion
  8.7 0.1 copy.45
  8.7 0.2 convolution_select_fusion.1.rank_ref
  8.9 0.0 copy-start.2
  8.9 0.2 select_reduce_fusion
  9.2 0.7 reshape.155.slots_ref
  9.8 0.8 convolution_select_fusion.rank_ref
  10.6 0.0 copy-done
  10.6 1.3 copy.49.wg_hbm
  11.9 0.0 copy-done.1
  11.9 1.3 copy.50.wu_hbm
  13.2 0.0 copy-done.2
  13.3 74.1 %attend.1.msg_ref = bf16[64,80,128]{2,1,0:T(8,128)(2,1)} custom-call(s32[512]{0:T(512)} %reshape.155.slots_ref, bf16[4,16,128]{2,1,0:T(8,128)(2,1)} %bitcast.29, f32[8,256]{1,0:T(8,128)} %copy-done.2, bf16[8,2048,128]{2,1,0:T(8,128)(2,1)} %bitcast.23, bf16[8,2048,128]{2,1,0:T(8,128)(2,1)} %bitcast.24), custom_call_target="tpu_custom_call" | custom-call | tf_op jit(solution)/shard_map/attend/pallas_call | solution.py:491
  87.3 71.8 %layer.1 = (bf16[16,512]{1,0:T(8,128)(2,1)}, bf16[16,512]{1,0:T(8,128)(2,1)}) custom-call(bf16[64,80,128]{2,1,0:T(8,128)(2,1)} %attend.1.msg_ref, f32[64,256]{1,0:T(8,128)} %convolution_select_fusion.rank_ref, bf16[16,512]{1,0:T(8,128)(2,1)} %reshape.159.residual_ref, f32[1,2048]{1,0:T(1,128)} %bitcast.33, bf16[128,2048]{1,0:T(8,128)(2,1)} %wo_hbm.1, ...), custom_call_target="tpu_custom_call" | custom-call | tf_op jit(solution)/shard_map/layer/pallas_call | solution.py:512
  159.1 1.3 reshape.161
  160.5 1.3 reshape.163
  (4 shorter events, 0.1 us)
Async XLA Ops:
  0.6 11.3 %copy-start.1 = (bf16[2048,224]{0,1:T(8,128)(2,1)S(1)}, bf16[2048,224]{0,1:T(8,128)(2,1)}, u32[]{:S(2)}) copy-start(bf16[2048,224]{0,1:T(8,128)(2,1)} %param.18) | copy-start | bytes 2752516
  0.6 10.0 %copy-start = (bf16[2048,224]{0,1:T(8,128)(2,1)S(1)}, bf16[2048,224]{0,1:T(8,128)(2,1)}, u32[]{:S(2)}) copy-start(bf16[2048,224]{0,1:T(8,128)(2,1)} %param.17) | copy-start | bytes 2752516
  8.9 4.3 %copy-start.2 = (f32[8,256]{1,0:T(8,128)}, f32[8,256]{1,0:T(8,128)S(1)}, u32[]{:S(2)}) copy-start(f32[8,256]{1,0:T(8,128)S(1)} %convolution_select_fusion.1.rank_ref) | copy-start | bytes 24580

commit v2 on v1

v2 whole, which is shorter than its diff:
```python
import functools
import math

import jax
import jax.numpy as jnp
from jax import lax
from jax.experimental import pallas as pl
from jax.experimental.pallas import tpu as pltpu
from jax.sharding import PartitionSpec as P

NX, NY, NZ, NK = 4, 4, 8, 2
CTX = NY * NZ * NK
ROWS, HEADS, GROUP, WIDTH = 256, 8, 8, 128
KEYS, SLOTS = 2048, 64
MODEL, LOCAL, UNITS = 8192, 2048, 224
MSG = SLOTS + 16
EPS = 1e-5
LOWEST = -1e30
SCALE = WIDTH**-0.5 * math.log2(math.e)
MESH = pl.DeviceIdType.MESH
VMEM_LIMIT = 56 * 1024 * 1024
F32, BF16 = jnp.float32, jnp.bfloat16


def place():
    c = lax.axis_index("ctx")
    x = lax.axis_index("mp")
    return c, x, c // (NZ * NK), (c // NK) % NZ, c % NK


def ctx_of(y, z, k):
    return (y * NZ + z) * NK + k


def remote(src, dst, send_sem, recv_sem, ctx, mp):
    return pltpu.make_async_remote_copy(
        src_ref=src,
        dst_ref=dst,
        send_sem=send_sem,
        recv_sem=recv_sem,
        device_id=(ctx, mp),
        device_id_type=MESH,
    )


def dot(a, b, da, db):
    return lax.dot_general(a, b, (((da,), (db,)), ((), ())), preferred_element_type=F32)


def hp_at(t, y):
    return ((y // 2 + t % 2) % 2) * 2 + (y % 2 + t // 2) % 2


def layer_kernel(
    own_ref, chosen_ref, residual_ref, gain_ref, keys_ref, values_ref, wo_hbm, wg_hbm, wu_hbm, wd_hbm,
    stream_ref, update_ref,
    qbuf, qpair, kbuf, vbuf, q32, o32, st32, sendbuf, msg, picked, ranks, plane, slots_vmem, slots,
    wo, wg, wu, wd, weight, stats, running, num_t, xmsg, att_t,
    core_out, core_in, y_out, y_in, z_out, z_in,
    z_all, x_all, gu32, gu_out, gu_in, hid,
    k_sem, v_sem, s_sem,
    qz_send, qz_recv, p2_send, p2_recv, p3_send, p3_recv, qc_send, qc_recv,
    a_send, a_recv,
    w_sem, x_send, x_recv,
    c_send, c_recv, y_send, y_recv, z_send, z_recv,
    gz_send, gz_recv, gy_send, gy_recv, gc_send, gc_recv,
    r_send, r_recv, h_send, h_recv,
):
    c, x, y, z, k = place()
    other = ctx_of(y, z, 1 - k)
    pending = []

    barrier = pltpu.get_barrier_semaphore()
    pl.semaphore_signal(barrier, inc=1, device_id=(other, x), device_id_type=MESH)
    for j in range(1, NX):
        pl.semaphore_signal(barrier, inc=1, device_id=(c, (x + j) % NX), device_id_type=MESH)
    for j in range(1, NY):
        pl.semaphore_signal(barrier, inc=1, device_id=(ctx_of((y + j) % NY, z, k), x), device_id_type=MESH)
    for j in range(1, NZ):
        pl.semaphore_signal(barrier, inc=1, device_id=(ctx_of(y, (z + j) % NZ, k), x), device_id_type=MESH)

    def load(t, carry):
        h = hp_at(t // 2, y) * 2 + t % 2
        pltpu.make_async_copy(keys_ref.at[h], kbuf.at[h], k_sem.at[h]).start()
        pltpu.make_async_copy(values_ref.at[h], vbuf.at[h], v_sem.at[h]).start()
        return carry

    row_a = ((k * NX + x) * NY + y) * NZ
    row_b = ((k * NY + y) * NX + x) * NZ
    qbuf[0:2, row_a + z] = own_ref[0:2]
    qbuf[2:4, row_b + z] = own_ref[2:4]
    pl.semaphore_wait(barrier, 1 + NX - 1 + NY - 1 + NZ - 1)

    arrivals = []
    for j in range(1, NZ):
        to = ctx_of(y, (z + j) % NZ, k)
        for half, row in ((0, row_a), (1, row_b)):
            ref = qbuf.at[pl.ds(2 * half, 2), row + z]
            cp = remote(ref, ref, qz_send.at[half, j - 1], qz_recv.at[half, j - 1], to, x)
            cp.start()
            arrivals.append(cp)
    pending += arrivals
    lax.fori_loop(0, HEADS, load, 0)

    r_in = lax.broadcasted_iota(jnp.int32, (ROWS, ROWS), 0)
    r_out = lax.broadcasted_iota(jnp.int32, (ROWS, ROWS), 1)
    moved = ((r_in // 64) * 32 + ((r_in // 8) % 8) * 4 + r_in % 4) + ((r_in // 4) % 2) * 128
    permute = jnp.where(moved == r_out, 1.0, 0.0).astype(BF16)
    before = jnp.where(r_in < r_out, 1.0, 0.0).astype(BF16)
    listed = chosen_ref[...].reshape(HEADS * 16, ROWS).astype(F32).astype(BF16)
    picked[...] = dot(listed, permute, 1, 0)
    own_id = (c * NX + x).astype(F32)
    found = [
        jnp.max(jnp.where(picked[h * 16 : h * 16 + 16, :] == own_id, 1.0, 0.0), axis=0, keepdims=True)
        for h in range(HEADS)
    ]
    member = jnp.concatenate(found, axis=0)
    ranks[...] = jnp.where(member > 0.5, dot(jnp.concatenate([member, member], axis=0).astype(BF16), before, 1, 0)[0:HEADS], -1.0)
    ids = (lax.broadcasted_iota(jnp.int32, (CTX, ROWS), 0) * NX + x).astype(F32)
    member = jnp.zeros((CTX, ROWS), F32)
    for i in range(16):
        row = picked[pl.ds((c // GROUP) * 16 + i, 1), :]
        member = jnp.maximum(member, jnp.where(row == ids, 1.0, 0.0))
    plane[...] = jnp.where(member > 0.5, dot(member.astype(BF16), before, 1, 0), -1.0)
    r8 = lax.broadcasted_iota(jnp.int32, (16, ROWS), 1)
    kk, yy, zz, mm = r8 // 128, (r8 // 32) % 4, (r8 // 4) % 8, r8 % 4
    pos_a = (((kk * NX + mm) * NY + yy) * NZ + zz).astype(F32).astype(BF16)
    pos_b = (((kk * NY + yy) * NX + mm) * NZ + zz).astype(F32).astype(BF16)
    spot = lax.broadcasted_iota(jnp.int32, (128, ROWS), 0).astype(F32)
    for h in range(HEADS):
        hit = jnp.where(spot == ranks[h : h + 1, :], 1.0, 0.0).astype(BF16)
        at = dot(pos_a if h < 4 else pos_b, hit, 1, 1)
        slots_vmem[h : h + 1, :] = at[0:1].astype(jnp.int32)
    to_scalar = pltpu.make_async_copy(slots_vmem, slots, s_sem)
    to_scalar.start()
    for cp in arrivals:
        cp.wait_recv()

    arrivals = []
    for j in range(1, 4):
        ref = qbuf.at[0:2, pl.ds(row_a, NZ)]
        cp = remote(ref, ref, p2_send.at[0, j - 1], p2_recv.at[0, j - 1], ctx_of((y + j) % NY, z, k), x)
        cp.start()
        arrivals.append(cp)
        ref = qbuf.at[2:4, pl.ds(row_b, NZ)]
        cp = remote(ref, ref, p2_send.at[1, j - 1], p2_recv.at[1, j - 1], c, (x + j) % NX)
        cp.start()
        arrivals.append(cp)
    pending += arrivals
    for cp in arrivals:
        cp.wait_recv()

    def block(hp, n):
        return qbuf.at[hp, pl.ds(n * 32, 32)]

    def pass_on(hp, n, j):
        return remote(block(hp, n), block(hp, n), qc_send.at[hp, j], qc_recv.at[hp, j], other, x)

    for i in range(2):
        for j in range(1, 4):
            hp = (y % 2 + i) % 2
            ref = block(hp, k * NX + x)
            remote(ref, ref, p3_send.at[hp, j - 1], p3_recv.at[hp, j - 1], c, (x + j) % NX).start()
            to = (y + j) % NY
            hp = 2 + (to % 2 + i) % 2
            ref = block(hp, k * NY + y)
            remote(ref, ref, p3_send.at[hp, j - 1], p3_recv.at[hp, j - 1], ctx_of(to, z, k), x).start()
    for hp in range(4):
        pass_on(hp, k * 4 + (x if hp < 2 else y), 0).start()

    def forward(hp):
        late = hp // 2
        for j in range(1, 4):
            n = k * 4 + (x * (1 - late) + y * late - j + 4) % 4
            ref = block(hp, n)
            remote(ref, ref, p3_send.at[hp, j - 1], p3_recv.at[hp, j - 1], other, x).wait_recv()
            pass_on(hp, n, j).start()

    forward(hp_at(0, y))
    forward(hp_at(1, y))
    to_scalar.wait()
    slot_iota = lax.broadcasted_iota(jnp.int32, (SLOTS, ROWS), 0).astype(F32)

    def head(h):
        hp = h // 2
        upper = (h % 2) == 1
        pltpu.make_async_copy(keys_ref.at[h], kbuf.at[h], k_sem.at[h]).wait()
        pltpu.make_async_copy(values_ref.at[h], vbuf.at[h], v_sem.at[h]).wait()

        def pick(i, carry):
            for u in range(8):
                s = i * 8 + u
                row = jnp.minimum(jnp.maximum(slots[h, s], 0), ROWS - 1)
                tile = qpair[row].astype(F32)
                q32[pl.ds(pl.multiple_of(s * 8, 8), 8), :] = jnp.where(upper, tile[8:16], tile[0:8])
            return carry

        lax.fori_loop(0, SLOTS // 8, pick, 0)

        for b in range(2):
            at = pl.ds(b * 256, 256)
            s = dot(q32[at, :].astype(BF16), kbuf[h], 1, 1)
            top = (jnp.max(s, axis=1, keepdims=True) * SCALE).astype(BF16).astype(F32)
            p = jnp.exp2(s * SCALE - top)
            total = jnp.sum(p, axis=1, keepdims=True)
            o32[at, :] = dot(p.astype(BF16), vbuf[h], 1, 0)
            lane = lax.broadcasted_iota(jnp.int32, (256, WIDTH), 1)
            st32[at, :] = jnp.where(lane == 0, top, total)

        hit = slot_iota == ranks[pl.ds(h, 1), :]
        for g in range(GROUP):
            n = h * GROUP + g
            sendbuf[n, 0:SLOTS, :] = o32[pl.ds(g, SLOTS, stride=GROUP), :].astype(BF16)
            st = st32[pl.ds(g, SLOTS, stride=GROUP), :]
            top = jnp.sum(jnp.where(hit, st[:, 0:1], 0.0), axis=0, keepdims=True)
            total = jnp.sum(jnp.where(hit, st[:, 1:2], 0.0), axis=0, keepdims=True)
            high = total.astype(BF16).astype(F32)
            low = total - high
            tile = jnp.concatenate(
                [
                    top[:, :128], top[:, 128:], high[:, :128], high[:, 128:],
                    low[:, :128], low[:, 128:], jnp.zeros((10, 128), F32),
                ],
                axis=0,
            )
            sendbuf[n, SLOTS:MSG, :] = tile.astype(BF16)

            @pl.when(n != c)
            def _():
                remote(sendbuf.at[n], msg.at[c], a_send.at[n], a_recv.at[c], n, x).start()

            @pl.when(n == c)
            def _():
                msg[c] = sendbuf[n]

    def pair(t, carry):
        hp = hp_at(t, y)
        for j in range(4):
            pass_on(hp, 0, j).wait_recv()
        qpair[...] = qbuf[hp]
        lax.fori_loop(0, 2, lambda i, v: (head(hp * 2 + i), v)[1], 0)

        @pl.when(t < 2)
        def _():
            forward(hp_at(t + 2, y))

        return carry

    lax.fori_loop(0, 4, pair, 0)

    loads = [
        pltpu.make_async_copy(wo_hbm, wo, w_sem.at[0]),
        pltpu.make_async_copy(wg_hbm, wg, w_sem.at[1]),
        pltpu.make_async_copy(wu_hbm, wu, w_sem.at[2]),
        pltpu.make_async_copy(wd_hbm, wd.at[pl.ds(0, UNITS)], w_sem.at[3]),
    ]
    for cp in loads:
        cp.start()
    wd[UNITS:256, :] = jnp.zeros((256 - UNITS, LOCAL), BF16)

    num_t[...] = jnp.zeros_like(num_t)
    running[0:1, :] = jnp.full((1, ROWS), LOWEST, F32)
    running[1:2, :] = jnp.zeros((1, ROWS), F32)

    def merge(t, carry):
        base = hp_at(t, y) * (NZ * NK)

        def arrive(i, v):
            s = base + i

            @pl.when(s != c)
            def _():
                remote(sendbuf.at[s], msg.at[s], a_send.at[s], a_recv.at[s], s, x).wait_recv()

            return v

        lax.fori_loop(0, NZ * NK, arrive, 0)
        for i in range(NZ * NK):
            stats[i * 16 : i * 16 + 16, :] = msg[base + i, SLOTS:MSG, :].astype(F32)

        def row_of(n):
            return jnp.concatenate([stats[pl.ds(2 * n + i, NZ * NK, stride=16), :] for i in range(2)], axis=1)

        rank = plane[pl.ds(pl.multiple_of(base, 16), 16), :]
        listed = rank >= 0.0
        top_each = jnp.where(listed, row_of(0), LOWEST)
        old = running[0:1, :]
        top = jnp.maximum(old, jnp.max(top_each, axis=0, keepdims=True))
        keep = jnp.exp2(old - top)
        w = jnp.where(listed, jnp.exp2(top_each - top), 0.0).astype(BF16).astype(F32)
        running[0:1, :] = top
        running[1:2, :] = running[1:2, :] * keep + jnp.sum(w * (row_of(1) + row_of(2)), axis=0, keepdims=True)
        total = num_t[...] * keep
        for i in range(NZ * NK // 4):
            for u in range(4):
                s = i * 4 + u
                weight[s * SLOTS : (s + 1) * SLOTS, :] = jnp.where(
                    slot_iota == rank[s : s + 1, :], w[s : s + 1, :], 0.0
                ).astype(BF16)
            values = jnp.concatenate([msg[base + i * 4 + u, 0:SLOTS, :] for u in range(4)], axis=0)
            total = total + dot(values, weight[i * 4 * SLOTS : (i + 1) * 4 * SLOTS, :], 0, 0)
        num_t[...] = total
        return carry

    lax.fori_loop(0, 4, merge, 0)

    top, den = running[0:1, :], running[1:2, :]

    xmsg[x, 0:WIDTH, :] = num_t[...].astype(BF16)
    den_high = den.astype(BF16).astype(F32)
    xmsg[x, WIDTH : WIDTH + 16, :] = jnp.concatenate(
        [top, den_high, den - den_high, jnp.zeros((13, ROWS), F32)], axis=0
    ).astype(BF16)
    arrivals = []
    for j in range(1, NX):
        cp = remote(xmsg.at[x], xmsg.at[x], x_send.at[j - 1], x_recv.at[j - 1], c, (x + j) % NX)
        cp.start()
        arrivals.append(cp)
    pending += arrivals
    for cp in arrivals:
        cp.wait_recv()
    tails = [xmsg[i, WIDTH : WIDTH + 16, :].astype(F32) for i in range(NX)]
    best = functools.reduce(jnp.maximum, [v[0:1] for v in tails])
    num, den = 0.0, 0.0
    for i in range(NX):
        f = jnp.exp2(tails[i][0:1] - best)
        den = den + f * (tails[i][1:2] + tails[i][2:3])
        num = num + f * xmsg[i, 0:WIDTH, :].astype(F32)
    att_t[...] = (num / den).astype(BF16)

    def half(v_ref, which):
        return v_ref[:, pl.ds(pl.multiple_of(which * 128, 128), 128)]

    def reduce_scatter(n, piece):
        core_out[n] = piece(1 - k).astype(BF16)
        cp = remote(core_out.at[n], core_in.at[n], c_send.at[n], c_recv.at[n], other, x)
        cp.start()
        mine = piece(k)
        cp.wait_recv()
        total = mine + core_in[n].astype(F32)
        y_out[n] = total.reshape(NY, 32, LOCAL).astype(BF16)
        pending.append(cp)
        arrivals = []
        for j in range(1, NY):
            to = (y + j) % NY
            cp = remote(y_out.at[n, to], y_in.at[n, j - 1], y_send.at[n, j - 1], y_recv.at[n, j - 1], ctx_of(to, z, k), x)
            cp.start()
            pending.append(cp)
            arrivals.append(cp)
        acc = y_out[n, y].astype(F32)
        for j, cp in enumerate(arrivals):
            cp.wait_recv()
            acc = acc + y_in[n, j].astype(F32)
        regroup(acc, z_out.at[n])
        arrivals = []
        for j in range(1, NZ):
            to = (z + j) % NZ
            cp = remote(z_out.at[n, to], z_in.at[n, j - 1], z_send.at[n, j - 1], z_recv.at[n, j - 1], ctx_of(y, to, k), x)
            cp.start()
            pending.append(cp)
            arrivals.append(cp)
        acc = z_out[n, z].astype(F32)
        for j, cp in enumerate(arrivals):
            cp.wait_recv()
            acc = acc + z_in[n, j].astype(F32)
        return acc

    loads[0].wait()
    projected = reduce_scatter(0, lambda which: dot(half(att_t, which), wo[...], 0, 0))
    stream = (fold(residual_ref[...].astype(F32)) + projected).astype(BF16)
    unfold(stream.astype(F32), stream_ref)

    z_all[z] = stream
    arrivals = []
    for j in range(1, NZ):
        cp = remote(z_all.at[z], z_all.at[z], gz_send.at[j - 1], gz_recv.at[j - 1], ctx_of(y, (z + j) % NZ, k), x)
        cp.start()
        pending.append(cp)
        arrivals.append(cp)
    for cp in arrivals:
        cp.wait_recv()

    def put(b, v):
        x_all[k, y, :, b * 512 : (b + 1) * 512] = v

    ungroup(z_all, put)
    arrivals = []
    for j in range(1, NY):
        cp = remote(x_all.at[k, y], x_all.at[k, y], gy_send.at[j - 1], gy_recv.at[j - 1], ctx_of((y + j) % NY, z, k), x)
        cp.start()
        pending.append(cp)
        arrivals.append(cp)
    for cp in arrivals:
        cp.wait_recv()
    core_copy = remote(x_all.at[k], x_all.at[k], gc_send, gc_recv, other, x)
    core_copy.start()
    pending.append(core_copy)
    loads[1].wait()
    loads[2].wait()

    def gate_up(which):
        rows = x_all[which].reshape(128, LOCAL)
        wide = rows.astype(F32)
        squares = jnp.sum(wide * wide, axis=1, keepdims=True)
        scaled = (wide * gain_ref[...]).astype(BF16)
        for n, weight_ref in enumerate((wg, wu)):
            gu32[n, which, :, 0:UNITS] = dot(scaled, weight_ref[...], 1, 1).astype(BF16)
        high = squares.astype(BF16).astype(F32)
        lane = lax.broadcasted_iota(jnp.int32, (128, 256 - UNITS), 1)
        gu32[0, which, :, UNITS:256] = jnp.where(lane == 0, high, squares - high).astype(BF16)
        gu32[1, which, :, UNITS:256] = jnp.zeros((128, 256 - UNITS), BF16)

    gate_up(k)
    core_copy.wait_recv()
    gate_up(1 - k)

    for q in range(NX):
        for n in range(2):
            gu_out[q, n] = gu32[n, q // 2, (q % 2) * 64 : (q % 2) * 64 + 64, :]
    arrivals = []
    for j in range(1, NX):
        to = (x + j) % NX
        cp = remote(gu_out.at[to], gu_in.at[j - 1], r_send.at[j - 1], r_recv.at[j - 1], c, to)
        cp.start()
        pending.append(cp)
        arrivals.append(cp)
    acc = gu_out[x].astype(F32)
    for j, cp in enumerate(arrivals):
        cp.wait_recv()
        acc = acc + gu_in[j].astype(F32)
    squares = acc[0, :, UNITS : UNITS + 1] + acc[0, :, UNITS + 1 : UNITS + 2]
    factor = lax.rsqrt(squares / MODEL + EPS)
    gate = acc[0] * factor
    up = acc[1] * factor
    lane = lax.broadcasted_iota(jnp.int32, (64, 256), 1)
    hidden = jnp.where(lane < UNITS, gate / (1.0 + jnp.exp(-gate)) * up, 0.0)
    hid[x] = hidden.astype(BF16)
    arrivals = []
    for j in range(1, NX):
        cp = remote(hid.at[x], hid.at[x], h_send.at[j - 1], h_recv.at[j - 1], c, (x + j) % NX)
        cp.start()
        pending.append(cp)
        arrivals.append(cp)
    for cp in arrivals:
        cp.wait_recv()
    loads[3].wait()

    def down(which):
        rows = hid[pl.ds(which * 2, 2)].reshape(128, 256)
        return dot(rows, wd[...], 1, 0)

    updated = reduce_scatter(1, down)
    unfold(updated, update_ref)
    for cp in pending:
        cp.wait_send()
    for hp in range(4):
        for j in range(3):
            remote(block(hp, 0), block(hp, 0), p3_send.at[hp, j], p3_recv.at[hp, j], other, x).wait_send()
        for j in range(4):
            pass_on(hp, 0, j).wait_send()

    def sent(n, carry):
        @pl.when(n != c)
        def _():
            remote(sendbuf.at[n], msg.at[n], a_send.at[n], a_recv.at[n], n, x).wait_send()

        return carry

    lax.fori_loop(0, CTX, sent, 0)

def swap4(v):
    return pltpu.roll(v, 4, 1)


def fold(v):
    return jnp.concatenate([v[:, b * 512 : (b + 1) * 512] for b in range(4)], axis=0)


def unfold(v, out_ref):
    for b in range(4):
        out_ref[:, b * 512 : (b + 1) * 512] = v[4 * b : 4 * b + 4].astype(BF16)


def regroup(acc, out_ref):
    parts = [acc[:, b * 512 : (b + 1) * 512].reshape(4, 8, 512) for b in range(4)]
    lower = lax.broadcasted_iota(jnp.int32, (4, 8, 512), 1) < 4
    even = [jnp.where(lower, parts[b], swap4(parts[b + 1])) for b in (0, 2)]
    odd = [jnp.where(lower, swap4(parts[b]), parts[b + 1]) for b in (0, 2)]
    for t in range(4):
        out_ref[2 * t] = jnp.concatenate([even[0][t], even[1][t]], axis=0).astype(BF16)
        out_ref[2 * t + 1] = jnp.concatenate([odd[0][t], odd[1][t]], axis=0).astype(BF16)


def ungroup(src_ref, store):
    a = src_ref[...].astype(F32)
    lower = lax.broadcasted_iota(jnp.int32, (8, 512), 0) < 4
    columns = [[], [], [], []]
    for t in range(4):
        for q in range(2):
            e = a[2 * t, 8 * q : 8 * q + 8]
            o = a[2 * t + 1, 8 * q : 8 * q + 8]
            columns[2 * q].append(jnp.where(lower, e, pltpu.roll(o, 4, 0)))
            columns[2 * q + 1].append(jnp.where(lower, pltpu.roll(e, 4, 0), o))
    for b in range(4):
        store(b, jnp.concatenate(columns[b], axis=0).astype(BF16))


def dma(*shape):
    return pltpu.SemaphoreType.DMA(shape)


def per_device(query, keys, values, chosen, residual, output_weight, norm_gain, gate_weight, up_weight, down_weight):
    vmem = pl.BlockSpec(memory_space=pltpu.VMEM)
    hbm = pl.BlockSpec(memory_space=pl.ANY)
    half = 16 * 16
    return pl.pallas_call(
        layer_kernel,
        out_shape=[jax.ShapeDtypeStruct((4, LOCAL), BF16)] * 2,
        in_specs=[vmem, vmem, vmem, vmem, hbm, hbm, hbm, hbm, hbm, hbm],
        out_specs=[vmem, vmem],
        scratch_shapes=[
            pltpu.VMEM((4, ROWS, 16, WIDTH), BF16),
            pltpu.VMEM((ROWS, 16, WIDTH), BF16),
            pltpu.VMEM((HEADS, KEYS, WIDTH), BF16),
            pltpu.VMEM((HEADS, KEYS, WIDTH), BF16),
            pltpu.VMEM((SLOTS * GROUP, WIDTH), F32),
            pltpu.VMEM((SLOTS * GROUP, WIDTH), F32),
            pltpu.VMEM((SLOTS * GROUP, WIDTH), F32),
            pltpu.VMEM((CTX, MSG, WIDTH), BF16),
            pltpu.VMEM((CTX, MSG, WIDTH), BF16),
            pltpu.VMEM((HEADS * 16, ROWS), F32),
            pltpu.VMEM((HEADS, ROWS), F32),
            pltpu.VMEM((CTX, ROWS), F32),
            pltpu.VMEM((HEADS, 128), jnp.int32),
            pltpu.SMEM((HEADS, 128), jnp.int32),
            pltpu.VMEM((WIDTH, LOCAL), BF16),
            pltpu.VMEM((UNITS, LOCAL), BF16),
            pltpu.VMEM((UNITS, LOCAL), BF16),
            pltpu.VMEM((256, LOCAL), BF16),
            pltpu.VMEM((16 * SLOTS, ROWS), BF16),
            pltpu.VMEM((half, WIDTH), F32),
            pltpu.VMEM((8, ROWS), F32),
            pltpu.VMEM((WIDTH, ROWS), F32),
            pltpu.VMEM((NX, WIDTH + 16, ROWS), BF16),
            pltpu.VMEM((WIDTH, ROWS), BF16),
            pltpu.VMEM((2, 128, LOCAL), BF16),
            pltpu.VMEM((2, 128, LOCAL), BF16),
            pltpu.VMEM((2, NY, 32, LOCAL), BF16),
            pltpu.VMEM((2, NY - 1, 32, LOCAL), BF16),
            pltpu.VMEM((2, NZ, 16, 512), BF16),
            pltpu.VMEM((2, NZ - 1, 16, 512), BF16),
            pltpu.VMEM((NZ, 16, 512), BF16),
            pltpu.VMEM((NK, NY, 32, LOCAL), BF16),
            pltpu.VMEM((2, NK, 128, 256), BF16),
            pltpu.VMEM((NX, 2, 64, 256), BF16),
            pltpu.VMEM((NX - 1, 2, 64, 256), BF16),
            pltpu.VMEM((NX, 64, 256), BF16),
            dma(HEADS), dma(HEADS), pltpu.SemaphoreType.DMA,
            dma(2, 7), dma(2, 7), dma(2, 3), dma(2, 3), dma(4, 3), dma(4, 3), dma(4, 4), dma(4, 4),
            dma(CTX), dma(CTX),
            dma(4), dma(3), dma(3),
            dma(2), dma(2), dma(2, 3), dma(2, 3), dma(2, 7), dma(2, 7),
            dma(7), dma(7), dma(3), dma(3), pltpu.SemaphoreType.DMA, pltpu.SemaphoreType.DMA,
            dma(3), dma(3), dma(3), dma(3),
        ],
        compiler_params=pltpu.CompilerParams(collective_id=0, has_side_effects=True, vmem_limit_bytes=VMEM_LIMIT),
        name="layer",
    )(
        query.reshape(4, 16, WIDTH), chosen.transpose(0, 2, 1), residual, norm_gain.reshape(1, LOCAL),
        keys[0], values[0], output_weight, gate_weight.T, up_weight.T, down_weight,
    )


def solution(mesh):
    return jax.shard_map(
        per_device,
        mesh=mesh,
        in_specs=(
            P(("ctx", "mp"), None, None, None),
            P(("ctx", "mp"), None, None, None),
            P(("ctx", "mp"), None, None, None),
            P(),
            P("ctx", "mp"),
            P("ctx", "mp"),
            P("mp"),
            P("mp", "ctx"),
            P("mp", "ctx"),
            P("ctx", "mp"),
        ),
        out_specs=(P("ctx", "mp"), P("ctx", "mp")),
        check_vma=False,
    )
```

time: 162 us -> 140 us (0.86)
  Pallas kernels: 146 us -> 136 us
  local copies, waits for them, and re-layouts: 9.13 us -> 2.66 us
  other arithmetic: 5.08 us -> 0 us
    pallas_call x2 -> x1, Pallas kernels: 146 us -> 136 us  [per_device(): pl.pallas_call(layer_kernel, out_shape=[jax.ShapeDtypeStruct((4, LOCAL),...]
    reshape x4 -> x0, local copies, waits for them, and re-layouts: 4.81 us -> none  [the longest x2 2.66 us: per_device(): unfold = lambda a: a.reshape(4, 4, 512).transpose(1, 0, 2).reshape(4, LOCAL)]
    reduce_or x2 -> x0, other arithmetic: 4.76 us -> none  [the longest x1 4.49 us: prelude(): own = ranks(jnp.any(ordered == p, axis=2))]
    unnamed x9 -> x2, local copies, waits for them, and re-layouts: 3.97 us -> 2.66 us
where the time goes in v2:
time: 140 us
  Pallas kernels  136 us (97%)
  local copies, waits for them, and re-layouts  2.66 us (2%)
    pallas_call x1, Pallas kernels, per_device(): pl.pallas_call(layer_kernel, out_shape=[jax.ShapeDtypeStruct((4, LOCAL),...  136 us

profile of v2, /device:TPU:1, one launch (start us, length us, event | category | flops | bytes accessed | tf_op | source)
XLA Modules:
  0.0 139.5 jit_solution(7568423406253324648)
XLA Ops:
  0.6 136.2 %layer.1 = (bf16[4,2048]{1,0:T(4,128)(2,1)}, bf16[4,2048]{1,0:T(4,128)(2,1)}) custom-call(bf16[4,16,128]{2,1,0:T(8,128)(2,1)} %bitcast.12, s32[8,16,256]{2,1,0:T(8,128)} %bitcast.11, bf16[4,2048]{1,0:T(4,128)(2,1)} %residual_ref.1, f32[1,2048]{1,0:T(1,128)} %bitcast.13, bf16[8,2048,128]{2,1,0:T(8,128)(2,1)} %bitcast.7, bf16[8,2048,128]{2,1,0:T(8,128)(2,1)} %bitcast.8, ...), custom_call_target="tpu_custom_call" | custom-call | tf_op jit(solution)/shard_map/layer/pallas_call | solution.py:516
  136.9 1.3 copy.14
  138.2 1.3 copy.15

commit v3 on v2

--- a/solution.py
+++ b/solution.py
@@ -12,7 +12,7 @@
 CTX = NY * NZ * NK
 ROWS, HEADS, GROUP, WIDTH = 256, 8, 8, 128
 KEYS, SLOTS = 2048, 64
-MODEL, LOCAL, UNITS = 8192, 2048, 224
+MODEL, LOCAL, HALF, UNITS = 8192, 2048, 1024, 224
 MSG = SLOTS + 16
 EPS = 1e-5
 LOWEST = -1e30
@@ -59,7 +59,7 @@
     core_out, core_in, y_out, y_in, z_out, z_in,
     z_all, x_all, gu32, gu_out, gu_in, hid,
     k_sem, v_sem, s_sem,
-    qz_send, qz_recv, p2_send, p2_recv, p3_send, p3_recv, qc_send, qc_recv,
+    qz_send, qz_recv, p2_send, p2_recv, p3_send, p3_recv, p4_send, p4_recv, qc_send, qc_recv,
     a_send, a_recv,
     w_sem, x_send, x_recv,
     c_send, c_recv, y_send, y_recv, z_send, z_recv,
@@ -101,6 +101,16 @@
             arrivals.append(cp)
     pending += arrivals
     lax.fori_loop(0, HEADS, load, 0)
+
+    loads = [
+        pltpu.make_async_copy(wo_hbm, wo, w_sem.at[0]),
+        pltpu.make_async_copy(wg_hbm, wg, w_sem.at[1]),
+        pltpu.make_async_copy(wu_hbm, wu, w_sem.at[2]),
+        pltpu.make_async_copy(wd_hbm, wd.at[pl.ds(0, UNITS)], w_sem.at[3]),
+    ]
+    for cp in loads:
+        cp.start()
+    wd[UNITS:256, :] = jnp.zeros((256 - UNITS, LOCAL), BF16)
 
     r_in = lax.broadcasted_iota(jnp.int32, (ROWS, ROWS), 0)
     r_out = lax.broadcasted_iota(jnp.int32, (ROWS, ROWS), 1)
@@ -147,8 +157,6 @@
         cp.start()
         arrivals.append(cp)
     pending += arrivals
-    for cp in arrivals:
-        cp.wait_recv()
 
     def block(hp, n):
         return qbuf.at[hp, pl.ds(n * 32, 32)]
@@ -156,28 +164,46 @@
     def pass_on(hp, n, j):
         return remote(block(hp, n), block(hp, n), qc_send.at[hp, j], qc_recv.at[hp, j], other, x)
 
-    for i in range(2):
+    def piece_of(hp, row, i, j):
+        ref = qbuf.at[hp, pl.ds(row, NZ)]
+        return ref, p4_send.at[hp, j - 1, i], p4_recv.at[hp, j - 1, i]
+
+    for i in range(4):
+        if i:
+            for cp in arrivals[2 * i - 2 : 2 * i]:
+                cp.wait_recv()
         for j in range(1, 4):
-            hp = (y % 2 + i) % 2
-            ref = block(hp, k * NX + x)
-            remote(ref, ref, p3_send.at[hp, j - 1], p3_recv.at[hp, j - 1], c, (x + j) % NX).start()
+            ref, send, recv = piece_of(y % 2, ((k * NX + x) * NY + (y - i + NY) % NY) * NZ, i, j)
+            remote(ref, ref, send, recv, c, (x + j) % NX).start()
             to = (y + j) % NY
-            hp = 2 + (to % 2 + i) % 2
-            ref = block(hp, k * NY + y)
-            remote(ref, ref, p3_send.at[hp, j - 1], p3_recv.at[hp, j - 1], ctx_of(to, z, k), x).start()
+            ref, send, recv = piece_of(2 + to % 2, ((k * NY + y) * NX + (x - i + NX) % NX) * NZ, i, j)
+            remote(ref, ref, send, recv, ctx_of(to, z, k), x).start()
+    for j in range(1, 4):
+        hp = (y % 2 + 1) % 2
+        ref = block(hp, k * NX + x)
+        remote(ref, ref, p3_send.at[hp, j - 1], p3_recv.at[hp, j - 1], c, (x + j) % NX).start()
+        to = (y + j) % NY
+        hp = 2 + (to % 2 + 1) % 2
+        ref = block(hp, k * NY + y)
+        remote(ref, ref, p3_send.at[hp, j - 1], p3_recv.at[hp, j - 1], ctx_of(to, z, k), x).start()
     for hp in range(4):
         pass_on(hp, k * 4 + (x if hp < 2 else y), 0).start()
 
-    def forward(hp):
+    def forward(hp, pieces):
         late = hp // 2
         for j in range(1, 4):
             n = k * 4 + (x * (1 - late) + y * late - j + 4) % 4
             ref = block(hp, n)
-            remote(ref, ref, p3_send.at[hp, j - 1], p3_recv.at[hp, j - 1], other, x).wait_recv()
+            if pieces:
+                for i in range(4):
+                    src, send, recv = piece_of(hp, n * 32, i, j)
+                    remote(src, src, send, recv, other, x).wait_recv()
+            else:
+                remote(ref, ref, p3_send.at[hp, j - 1], p3_recv.at[hp, j - 1], other, x).wait_recv()
             pass_on(hp, n, j).start()
 
-    forward(hp_at(0, y))
-    forward(hp_at(1, y))
+    forward(hp_at(0, y), True)
+    forward(hp_at(1, y), True)
     to_scalar.wait()
     slot_iota = lax.broadcasted_iota(jnp.int32, (SLOTS, ROWS), 0).astype(F32)
 
@@ -242,21 +268,11 @@
 
         @pl.when(t < 2)
         def _():
-            forward(hp_at(t + 2, y))
+            forward(hp_at(t + 2, y), False)
 
         return carry
 
     lax.fori_loop(0, 4, pair, 0)
-
-    loads = [
-        pltpu.make_async_copy(wo_hbm, wo, w_sem.at[0]),
-        pltpu.make_async_copy(wg_hbm, wg, w_sem.at[1]),
-        pltpu.make_async_copy(wu_hbm, wu, w_sem.at[2]),
-        pltpu.make_async_copy(wd_hbm, wd.at[pl.ds(0, UNITS)], w_sem.at[3]),
-    ]
-    for cp in loads:
-        cp.start()
-    wd[UNITS:256, :] = jnp.zeros((256 - UNITS, LOCAL), BF16)
 
     num_t[...] = jnp.zeros_like(num_t)
     running[0:1, :] = jnp.full((1, ROWS), LOWEST, F32)
@@ -331,92 +347,114 @@
     def half(v_ref, which):
         return v_ref[:, pl.ds(pl.multiple_of(which * 128, 128), 128)]
 
-    def reduce_scatter(n, piece):
-        core_out[n] = piece(1 - k).astype(BF16)
-        cp = remote(core_out.at[n], core_in.at[n], c_send.at[n], c_recv.at[n], other, x)
-        cp.start()
-        mine = piece(k)
-        cp.wait_recv()
-        total = mine + core_in[n].astype(F32)
-        y_out[n] = total.reshape(NY, 32, LOCAL).astype(BF16)
-        pending.append(cp)
-        arrivals = []
+    def reduce_scatter(n, piece, use):
+        cores, along_y, along_z = [], [], []
+        for h in range(2):
+            core_out[n, h] = piece(1 - k, h).astype(BF16)
+            cp = remote(core_out.at[n, h], core_in.at[n, h], c_send.at[n, h], c_recv.at[n, h], other, x)
+            cp.start()
+            cores.append(cp)
+        for h in range(2):
+            mine = piece(k, h)
+            cores[h].wait_recv()
+            total = mine + core_in[n, h].astype(F32)
+            y_out[n, h] = total.reshape(NY, 32, HALF).astype(BF16)
+            copies = []
+            for j in range(1, NY):
+                to = (y + j) % NY
+                cp = remote(
+                    y_out.at[n, h, to], y_in.at[n, h, j - 1], y_send.at[n, h, j - 1], y_recv.at[n, h, j - 1], ctx_of(to, z, k), x
+                )
+                cp.start()
+                copies.append(cp)
+            along_y.append(copies)
+        for h in range(2):
+            acc = y_out[n, h, y].astype(F32)
+            for j, cp in enumerate(along_y[h]):
+                cp.wait_recv()
+                acc = acc + y_in[n, h, j].astype(F32)
+            regroup(acc, z_out.at[n, h])
+            copies = []
+            for j in range(1, NZ):
+                to = (z + j) % NZ
+                cp = remote(
+                    z_out.at[n, h, to], z_in.at[n, h, j - 1], z_send.at[n, h, j - 1], z_recv.at[n, h, j - 1], ctx_of(y, to, k), x
+                )
+                cp.start()
+                copies.append(cp)
+            along_z.append(copies)
+        for h in range(2):
+            acc = z_out[n, h, z].astype(F32)
+            for j, cp in enumerate(along_z[h]):
+                cp.wait_recv()
+                acc = acc + z_in[n, h, j].astype(F32)
+            use(h, acc)
+        for copies in [cores] + along_y + along_z:
+            pending.extend(copies)
+
+    rows_z, rows_y, rows_c = [], [], []
+
+    def spread(h, projected):
+        stream = (fold(residual_ref[:, h * HALF : (h + 1) * HALF].astype(F32)) + projected).astype(BF16)
+        z_all[h, z] = stream
+        for j in range(1, NZ):
+            cp = remote(z_all.at[h, z], z_all.at[h, z], gz_send.at[h, j - 1], gz_recv.at[h, j - 1], ctx_of(y, (z + j) % NZ, k), x)
+            cp.start()
+            rows_z.append(cp)
+        unfold(stream.astype(F32), stream_ref, h)
+
+    loads[0].wait()
+    reduce_scatter(0, lambda which, h: dot(half(att_t, which), wo[:, h * HALF : (h + 1) * HALF], 0, 0), spread)
+    for h in range(2):
+        for cp in rows_z[h * (NZ - 1) : (h + 1) * (NZ - 1)]:
+            cp.wait_recv()
+
+        def put(b, v):
+            x_all[h, k, y, :, b * 256 : (b + 1) * 256] = v
+
+        ungroup(z_all.at[h], put)
         for j in range(1, NY):
-            to = (y + j) % NY
-            cp = remote(y_out.at[n, to], y_in.at[n, j - 1], y_send.at[n, j - 1], y_recv.at[n, j - 1], ctx_of(to, z, k), x)
+            ref = x_all.at[h, k, y]
+            cp = remote(ref, ref, gy_send.at[h, j - 1], gy_recv.at[h, j - 1], ctx_of((y + j) % NY, z, k), x)
             cp.start()
-            pending.append(cp)
-            arrivals.append(cp)
-        acc = y_out[n, y].astype(F32)
-        for j, cp in enumerate(arrivals):
-            cp.wait_recv()
-            acc = acc + y_in[n, j].astype(F32)
-        regroup(acc, z_out.at[n])
-        arrivals = []
-        for j in range(1, NZ):
-            to = (z + j) % NZ
-            cp = remote(z_out.at[n, to], z_in.at[n, j - 1], z_send.at[n, j - 1], z_recv.at[n, j - 1], ctx_of(y, to, k), x)
-            cp.start()
-            pending.append(cp)
-            arrivals.append(cp)
-        acc = z_out[n, z].astype(F32)
-        for j, cp in enumerate(arrivals):
-            cp.wait_recv()
-            acc = acc + z_in[n, j].astype(F32)
-        return acc
-
-    loads[0].wait()
-    projected = reduce_scatter(0, lambda which: dot(half(att_t, which), wo[...], 0, 0))
-    stream = (fold(residual_ref[...].astype(F32)) + projected).astype(BF16)
-    unfold(stream.astype(F32), stream_ref)
-
-    z_all[z] = stream
-    arrivals = []
-    for j in range(1, NZ):
-        cp = remote(z_all.at[z], z_all.at[z], gz_send.at[j - 1], gz_recv.at[j - 1], ctx_of(y, (z + j) % NZ, k), x)
-        cp.start()
-        pending.append(cp)
-        arrivals.append(cp)
-    for cp in arrivals:
-        cp.wait_recv()
-
-    def put(b, v):
-        x_all[k, y, :, b * 512 : (b + 1) * 512] = v
-
-    ungroup(z_all, put)
-    arrivals = []
-    for j in range(1, NY):
-        cp = remote(x_all.at[k, y], x_all.at[k, y], gy_send.at[j - 1], gy_recv.at[j - 1], ctx_of((y + j) % NY, z, k), x)
-        cp.start()
-        pending.append(cp)
-        arrivals.append(cp)
-    for cp in arrivals:
-        cp.wait_recv()
-    core_copy = remote(x_all.at[k], x_all.at[k], gc_send, gc_recv, other, x)
-    core_copy.start()
-    pending.append(core_copy)
+            rows_y.append(cp)
+
+    def gate_up(which, h):
+        wide = x_all[h, which].reshape(128, HALF).astype(F32)
+        squares = jnp.sum(wide * wide, axis=1, keepdims=True)
+        cut = slice(h * HALF, (h + 1) * HALF)
+        scaled = (wide * gain_ref[:, cut]).astype(BF16)
+        lane = lax.broadcasted_iota(jnp.int32, (128, 256 - UNITS), 1)
+        parts = [dot(scaled, weight_ref[:, cut], 1, 1) for weight_ref in (wg, wu)]
+        if h == 0:
+            for n in range(2):
+                gu32[n, which, :, 0:UNITS] = parts[n]
+            gu32[0, which, :, UNITS:256] = jnp.where(lane < 2, squares, 0.0)
+            gu32[1, which, :, UNITS:256] = jnp.zeros((128, 256 - UNITS), F32)
+        else:
+            for n in range(2):
+                gu32[n, which, :, 0:UNITS] += parts[n]
+            squares = squares + gu32[0, which, :, UNITS : UNITS + 1]
+            high = squares.astype(BF16).astype(F32)
+            gu32[0, which, :, UNITS:256] = jnp.where(lane == 0, high, squares - high)
+
     loads[1].wait()
     loads[2].wait()
-
-    def gate_up(which):
-        rows = x_all[which].reshape(128, LOCAL)
-        wide = rows.astype(F32)
-        squares = jnp.sum(wide * wide, axis=1, keepdims=True)
-        scaled = (wide * gain_ref[...]).astype(BF16)
-        for n, weight_ref in enumerate((wg, wu)):
-            gu32[n, which, :, 0:UNITS] = dot(scaled, weight_ref[...], 1, 1).astype(BF16)
-        high = squares.astype(BF16).astype(F32)
-        lane = lax.broadcasted_iota(jnp.int32, (128, 256 - UNITS), 1)
-        gu32[0, which, :, UNITS:256] = jnp.where(lane == 0, high, squares - high).astype(BF16)
-        gu32[1, which, :, UNITS:256] = jnp.zeros((128, 256 - UNITS), BF16)
-
-    gate_up(k)
-    core_copy.wait_recv()
-    gate_up(1 - k)
+    for h in range(2):
+        for cp in rows_y[h * (NY - 1) : (h + 1) * (NY - 1)]:
+            cp.wait_recv()
+        cp = remote(x_all.at[h, k], x_all.at[h, k], gc_send.at[h], gc_recv.at[h], other, x)
+        cp.start()
+        rows_c.append(cp)
+        gate_up(k, h)
+    for h in range(2):
+        rows_c[h].wait_recv()
+        gate_up(1 - k, h)
+    pending += rows_z + rows_y + rows_c
 
     for q in range(NX):
         for n in range(2):
-            gu_out[q, n] = gu32[n, q // 2, (q % 2) * 64 : (q % 2) * 64 + 64, :]
+            gu_out[q, n] = gu32[n, q // 2, (q % 2) * 64 : (q % 2) * 64 + 64, :].astype(BF16)
     arrivals = []
     for j in range(1, NX):
         to = (x + j) % NX
@@ -445,17 +483,22 @@
         cp.wait_recv()
     loads[3].wait()
 
-    def down(which):
+    def down(which, h):
         rows = hid[pl.ds(which * 2, 2)].reshape(128, 256)
-        return dot(rows, wd[...], 1, 0)
-
-    updated = reduce_scatter(1, down)
-    unfold(updated, update_ref)
+        return dot(rows, wd[:, h * HALF : (h + 1) * HALF], 1, 0)
+
+    reduce_scatter(1, down, lambda h, total: unfold(total, update_ref, h))
     for cp in pending:
         cp.wait_send()
+    for j in range(1, 4):
+        to = (y + j) % NY
+        for first in (y % 2, 2 + to % 2):
+            for i in range(4):
+                src, send, recv = piece_of(first, 0, i, j)
+                remote(src, src, send, recv, other, x).wait_send()
+        for hp in ((y % 2 + 1) % 2, 2 + (to % 2 + 1) % 2):
+            remote(block(hp, 0), block(hp, 0), p3_send.at[hp, j - 1], p3_recv.at[hp, j - 1], other, x).wait_send()
     for hp in range(4):
-        for j in range(3):
-            remote(block(hp, 0), block(hp, 0), p3_send.at[hp, j], p3_recv.at[hp, j], other, x).wait_send()
         for j in range(4):
             pass_on(hp, 0, j).wait_send()
 
@@ -473,17 +516,18 @@
 
 
 def fold(v):
-    return jnp.concatenate([v[:, b * 512 : (b + 1) * 512] for b in range(4)], axis=0)
-
-
-def unfold(v, out_ref):
+    return jnp.concatenate([v[:, b * 256 : (b + 1) * 256] for b in range(4)], axis=0)
+
+
+def unfold(v, out_ref, h):
     for b in range(4):
-        out_ref[:, b * 512 : (b + 1) * 512] = v[4 * b : 4 * b + 4].astype(BF16)
+        at = h * HALF + b * 256
+        out_ref[:, at : at + 256] = v[4 * b : 4 * b + 4].astype(BF16)
 
 
 def regroup(acc, out_ref):
-    parts = [acc[:, b * 512 : (b + 1) * 512].reshape(4, 8, 512) for b in range(4)]
-    lower = lax.broadcasted_iota(jnp.int32, (4, 8, 512), 1) < 4
+    parts = [acc[:, b * 256 : (b + 1) * 256].reshape(4, 8, 256) for b in range(4)]
+    lower = lax.broadcasted_iota(jnp.int32, (4, 8, 256), 1) < 4
     even = [jnp.where(lower, parts[b], swap4(parts[b + 1])) for b in (0, 2)]
     odd = [jnp.where(lower, swap4(parts[b]), parts[b + 1]) for b in (0, 2)]
     for t in range(4):
@@ -493,7 +537,7 @@
 
 def ungroup(src_ref, store):
     a = src_ref[...].astype(F32)
-    lower = lax.broadcasted_iota(jnp.int32, (8, 512), 0) < 4
+    lower = lax.broadcasted_iota(jnp.int32, (8, 256), 0) < 4
     columns = [[], [], [], []]
     for t in range(4):
         for q in range(2):
@@ -505,6 +549,11 @@
         store(b, jnp.concatenate(columns[b], axis=0).astype(BF16))
 
 
+def hand_out(stream_in, update_in, stream_ref, update_ref):
+    stream_ref[...] = stream_in[...]
+    update_ref[...] = update_in[...]
+
+
 def dma(*shape):
     return pltpu.SemaphoreType.DMA(shape)
 
@@ -513,7 +562,7 @@
     vmem = pl.BlockSpec(memory_space=pltpu.VMEM)
     hbm = pl.BlockSpec(memory_space=pl.ANY)
     half = 16 * 16
-    return pl.pallas_call(
+    stream, update = pl.pallas_call(
         layer_kernel,
         out_shape=[jax.ShapeDtypeStruct((4, LOCAL), BF16)] * 2,
         in_specs=[vmem, vmem, vmem, vmem, hbm, hbm, hbm, hbm, hbm, hbm],
@@ -543,24 +592,24 @@
             pltpu.VMEM((WIDTH, ROWS), F32),
             pltpu.VMEM((NX, WIDTH + 16, ROWS), BF16),
             pltpu.VMEM((WIDTH, ROWS), BF16),
-            pltpu.VMEM((2, 128, LOCAL), BF16),
-            pltpu.VMEM((2, 128, LOCAL), BF16),
-            pltpu.VMEM((2, NY, 32, LOCAL), BF16),
-            pltpu.VMEM((2, NY - 1, 32, LOCAL), BF16),
-            pltpu.VMEM((2, NZ, 16, 512), BF16),
-            pltpu.VMEM((2, NZ - 1, 16, 512), BF16),
-            pltpu.VMEM((NZ, 16, 512), BF16),
-            pltpu.VMEM((NK, NY, 32, LOCAL), BF16),
-            pltpu.VMEM((2, NK, 128, 256), BF16),
+            pltpu.VMEM((2, 2, 128, HALF), BF16),
+            pltpu.VMEM((2, 2, 128, HALF), BF16),
+            pltpu.VMEM((2, 2, NY, 32, HALF), BF16),
+            pltpu.VMEM((2, 2, NY - 1, 32, HALF), BF16),
+            pltpu.VMEM((2, 2, NZ, 16, 256), BF16),
+            pltpu.VMEM((2, 2, NZ - 1, 16, 256), BF16),
+            pltpu.VMEM((2, NZ, 16, 256), BF16),
+            pltpu.VMEM((2, NK, NY, 32, HALF), BF16),
+            pltpu.VMEM((2, NK, 128, 256), F32),
             pltpu.VMEM((NX, 2, 64, 256), BF16),
             pltpu.VMEM((NX - 1, 2, 64, 256), BF16),
             pltpu.VMEM((NX, 64, 256), BF16),
             dma(HEADS), dma(HEADS), pltpu.SemaphoreType.DMA,
-            dma(2, 7), dma(2, 7), dma(2, 3), dma(2, 3), dma(4, 3), dma(4, 3), dma(4, 4), dma(4, 4),
+            dma(2, 7), dma(2, 7), dma(2, 3), dma(2, 3), dma(4, 3), dma(4, 3), dma(4, 3, 4), dma(4, 3, 4), dma(4, 4), dma(4, 4),
             dma(CTX), dma(CTX),
             dma(4), dma(3), dma(3),
-            dma(2), dma(2), dma(2, 3), dma(2, 3), dma(2, 7), dma(2, 7),
-            dma(7), dma(7), dma(3), dma(3), pltpu.SemaphoreType.DMA, pltpu.SemaphoreType.DMA,
+            dma(2, 2), dma(2, 2), dma(2, 2, 3), dma(2, 2, 3), dma(2, 2, 7), dma(2, 2, 7),
+            dma(2, 7), dma(2, 7), dma(2, 3), dma(2, 3), dma(2), dma(2),
             dma(3), dma(3), dma(3), dma(3),
         ],
         compiler_params=pltpu.CompilerParams(collective_id=0, has_side_effects=True, vmem_limit_bytes=VMEM_LIMIT),
@@ -569,6 +618,13 @@
         query.reshape(4, 16, WIDTH), chosen.transpose(0, 2, 1), residual, norm_gain.reshape(1, LOCAL),
         keys[0], values[0], output_weight, gate_weight.T, up_weight.T, down_weight,
     )
+    return pl.pallas_call(
+        hand_out,
+        out_shape=[jax.ShapeDtypeStruct((4, LOCAL), BF16)] * 2,
+        in_specs=[vmem, vmem],
+        out_specs=[vmem, vmem],
+        name="hand_out",
+    )(stream, update)
 
 
 def solution(mesh):

time: 140 us -> 132 us (0.943)
  Pallas kernels: 136 us -> 131 us
  local copies, waits for them, and re-layouts: 2.66 us -> 0 us
    pallas_call x1, Pallas kernels: 136 us -> 129 us  [per_device(): pl.pallas_call(layer_kernel, out_shape=[jax.ShapeDtypeStruct((4, LOCAL),...]
    unnamed x2 -> x0, local copies, waits for them, and re-layouts: 2.66 us -> none
where the time goes in v3:
time: 132 us; the launch traced here: 131 us
  Pallas kernels  131 us (99%)
    pallas_call x1, Pallas kernels, per_device(): pl.pallas_call(layer_kernel, out_shape=[jax.ShapeDtypeStruct((4, LOCAL),...  129 us

profile of v3, /device:TPU:1, one launch (start us, length us, event | category | flops | bytes accessed | tf_op | source)
XLA Modules:
  0.0 131.4 jit_solution(8761131812037203156)
XLA Ops:
  0.6 129.4 %layer.1 = (bf16[4,2048]{1,0:T(4,128)(2,1)}, bf16[4,2048]{1,0:T(4,128)(2,1)}) custom-call(bf16[4,16,128]{2,1,0:T(8,128)(2,1)} %bitcast.12, s32[8,16,256]{2,1,0:T(8,128)} %bitcast.11, bf16[4,2048]{1,0:T(4,128)(2,1)} %residual_ref.1, f32[1,2048]{1,0:T(1,128)} %bitcast.13, bf16[8,2048,128]{2,1,0:T(8,128)(2,1)} %bitcast.7, bf16[8,2048,128]{2,1,0:T(8,128)(2,1)} %bitcast.8, ...), custom_call_target="tpu_custom_call" | custom-call | tf_op jit(solution)/shard_map/layer/pallas_call | solution.py:565
  130.0 1.3 %hand_out.1 = (bf16[4,2048]{1,0:T(4,128)(2,1)}, bf16[4,2048]{1,0:T(4,128)(2,1)}) custom-call(bf16[4,2048]{1,0:T(4,128)(2,1)} %get-tuple-element.4.stream_in, bf16[4,2048]{1,0:T(4,128)(2,1)} %get-tuple-element.5.update_in), custom_call_target="tpu_custom_call" | custom-call | tf_op jit(solution)/shard_map/hand_out/pallas_call | solution.py:621

commit v4 on v3

--- a/solution.py
+++ b/solution.py
@@ -13,7 +13,6 @@
 ROWS, HEADS, GROUP, WIDTH = 256, 8, 8, 128
 KEYS, SLOTS = 2048, 64
 MODEL, LOCAL, HALF, UNITS = 8192, 2048, 1024, 224
-MSG = SLOTS + 16
 EPS = 1e-5
 LOWEST = -1e30
 SCALE = WIDTH**-0.5 * math.log2(math.e)
@@ -52,15 +51,15 @@
 
 
 def layer_kernel(
-    own_ref, chosen_ref, residual_ref, gain_ref, keys_ref, values_ref, wo_hbm, wg_hbm, wu_hbm, wd_hbm,
+    own_hbm, chosen_hbm, residual_ref, gain_hbm, keys_ref, values_ref, wo_hbm, wg_hbm, wu_hbm, wd_hbm,
     stream_ref, update_ref,
-    qbuf, qpair, kbuf, vbuf, q32, o32, st32, sendbuf, msg, picked, ranks, plane, slots_vmem, slots,
+    own_ref, chosen_ref, gain_ref, qbuf, qpair, kbuf, vbuf, q32, o32, st32, sendbuf, msg, tops_out, tops_in, picked, ranks, plane, slots_vmem, slots,
     wo, wg, wu, wd, weight, stats, running, num_t, xmsg, att_t,
     core_out, core_in, y_out, y_in, z_out, z_in,
     z_all, x_all, gu32, gu_out, gu_in, hid,
     k_sem, v_sem, s_sem,
     qz_send, qz_recv, p2_send, p2_recv, p3_send, p3_recv, p4_send, p4_recv, qc_send, qc_recv,
-    a_send, a_recv,
+    a_send, a_recv, b_send, b_recv, i_sem,
     w_sem, x_send, x_recv,
     c_send, c_recv, y_send, y_recv, z_send, z_recv,
     gz_send, gz_recv, gy_send, gy_recv, gc_send, gc_recv,
@@ -87,6 +86,14 @@
 
     row_a = ((k * NX + x) * NY + y) * NZ
     row_b = ((k * NY + y) * NX + x) * NZ
+    given = [
+        pltpu.make_async_copy(own_hbm, own_ref, i_sem.at[0]),
+        pltpu.make_async_copy(chosen_hbm, chosen_ref, i_sem.at[1]),
+        pltpu.make_async_copy(gain_hbm, gain_ref, i_sem.at[2]),
+    ]
+    for cp in given:
+        cp.start()
+    given[0].wait()
     qbuf[0:2, row_a + z] = own_ref[0:2]
     qbuf[2:4, row_b + z] = own_ref[2:4]
     pl.semaphore_wait(barrier, 1 + NX - 1 + NY - 1 + NZ - 1)
@@ -111,6 +118,9 @@
     for cp in loads:
         cp.start()
     wd[UNITS:256, :] = jnp.zeros((256 - UNITS, LOCAL), BF16)
+
+    for cp in given[1:]:
+        cp.wait()
 
     r_in = lax.broadcasted_iota(jnp.int32, (ROWS, ROWS), 0)
     r_out = lax.broadcasted_iota(jnp.int32, (ROWS, ROWS), 1)
@@ -233,31 +243,24 @@
             lane = lax.broadcasted_iota(jnp.int32, (256, WIDTH), 1)
             st32[at, :] = jnp.where(lane == 0, top, total)
 
-        hit = slot_iota == ranks[pl.ds(h, 1), :]
+        lane = lax.broadcasted_iota(jnp.int32, (SLOTS, WIDTH), 1)
+        slot = lax.broadcasted_iota(jnp.int32, (SLOTS, WIDTH), 0)
         for g in range(GROUP):
             n = h * GROUP + g
-            sendbuf[n, 0:SLOTS, :] = o32[pl.ds(g, SLOTS, stride=GROUP), :].astype(BF16)
+            sendbuf[n] = o32[pl.ds(g, SLOTS, stride=GROUP), :].astype(BF16)
             st = st32[pl.ds(g, SLOTS, stride=GROUP), :]
-            top = jnp.sum(jnp.where(hit, st[:, 0:1], 0.0), axis=0, keepdims=True)
-            total = jnp.sum(jnp.where(hit, st[:, 1:2], 0.0), axis=0, keepdims=True)
-            high = total.astype(BF16).astype(F32)
-            low = total - high
-            tile = jnp.concatenate(
-                [
-                    top[:, :128], top[:, 128:], high[:, :128], high[:, 128:],
-                    low[:, :128], low[:, 128:], jnp.zeros((10, 128), F32),
-                ],
-                axis=0,
-            )
-            sendbuf[n, SLOTS:MSG, :] = tile.astype(BF16)
+            spread = jnp.where(lane == slot, st[:, 0:1], jnp.where(lane == slot + SLOTS, st[:, 1:2], 0.0))
+            tops_out[n] = jnp.sum(spread, axis=0, keepdims=True)
 
             @pl.when(n != c)
             def _():
                 remote(sendbuf.at[n], msg.at[c], a_send.at[n], a_recv.at[c], n, x).start()
+                remote(tops_out.at[n], tops_in.at[c], b_send.at[n], b_recv.at[c], n, x).start()
 
             @pl.when(n == c)
             def _():
                 msg[c] = sendbuf[n]
+                tops_in[c] = tops_out[n]
 
     def pair(t, carry):
         hp = hp_at(t, y)
@@ -287,25 +290,34 @@
             @pl.when(s != c)
             def _():
                 remote(sendbuf.at[s], msg.at[s], a_send.at[s], a_recv.at[s], s, x).wait_recv()
+                remote(tops_out.at[s], tops_in.at[s], b_send.at[s], b_recv.at[s], s, x).wait_recv()
 
             return v
 
         lax.fori_loop(0, NZ * NK, arrive, 0)
         for i in range(NZ * NK):
-            stats[i * 16 : i * 16 + 16, :] = msg[base + i, SLOTS:MSG, :].astype(F32)
-
-        def row_of(n):
-            return jnp.concatenate([stats[pl.ds(2 * n + i, NZ * NK, stride=16), :] for i in range(2)], axis=1)
-
+            stats[i : i + 1, :] = tops_in[base + i]
+        held = stats[...]
         rank = plane[pl.ds(pl.multiple_of(base, 16), 16), :]
+        at = jnp.maximum(rank, 0.0).astype(jnp.int32)
+
+        def by_row(first):
+            return jnp.concatenate(
+                [
+                    jnp.take_along_axis(held, at[:, i * 128 : (i + 1) * 128] + first, axis=1, mode="promise_in_bounds")
+                    for i in range(2)
+                ],
+                axis=1,
+            )
+
         listed = rank >= 0.0
-        top_each = jnp.where(listed, row_of(0), LOWEST)
+        top_each = jnp.where(listed, by_row(0), LOWEST)
         old = running[0:1, :]
         top = jnp.maximum(old, jnp.max(top_each, axis=0, keepdims=True))
         keep = jnp.exp2(old - top)
         w = jnp.where(listed, jnp.exp2(top_each - top), 0.0).astype(BF16).astype(F32)
         running[0:1, :] = top
-        running[1:2, :] = running[1:2, :] * keep + jnp.sum(w * (row_of(1) + row_of(2)), axis=0, keepdims=True)
+        running[1:2, :] = running[1:2, :] * keep + jnp.sum(w * by_row(SLOTS), axis=0, keepdims=True)
         total = num_t[...] * keep
         for i in range(NZ * NK // 4):
             for u in range(4):
@@ -313,7 +325,7 @@
                 weight[s * SLOTS : (s + 1) * SLOTS, :] = jnp.where(
                     slot_iota == rank[s : s + 1, :], w[s : s + 1, :], 0.0
                 ).astype(BF16)
-            values = jnp.concatenate([msg[base + i * 4 + u, 0:SLOTS, :] for u in range(4)], axis=0)
+            values = jnp.concatenate([msg[base + i * 4 + u] for u in range(4)], axis=0)
             total = total + dot(values, weight[i * 4 * SLOTS : (i + 1) * 4 * SLOTS, :], 0, 0)
         num_t[...] = total
         return carry
@@ -506,6 +518,7 @@
         @pl.when(n != c)
         def _():
             remote(sendbuf.at[n], msg.at[n], a_send.at[n], a_recv.at[n], n, x).wait_send()
+            remote(tops_out.at[n], tops_in.at[n], b_send.at[n], b_recv.at[n], n, x).wait_send()
 
         return carry
 
@@ -561,13 +574,15 @@
 def per_device(query, keys, values, chosen, residual, output_weight, norm_gain, gate_weight, up_weight, down_weight):
     vmem = pl.BlockSpec(memory_space=pltpu.VMEM)
     hbm = pl.BlockSpec(memory_space=pl.ANY)
-    half = 16 * 16
     stream, update = pl.pallas_call(
         layer_kernel,
         out_shape=[jax.ShapeDtypeStruct((4, LOCAL), BF16)] * 2,
-        in_specs=[vmem, vmem, vmem, vmem, hbm, hbm, hbm, hbm, hbm, hbm],
+        in_specs=[hbm, hbm, vmem, hbm, hbm, hbm, hbm, hbm, hbm, hbm],
         out_specs=[vmem, vmem],
         scratch_shapes=[
+            pltpu.VMEM((4, 16, WIDTH), BF16),
+            pltpu.VMEM((HEADS, 16, ROWS), jnp.int32),
+            pltpu.VMEM((1, LOCAL), F32),
             pltpu.VMEM((4, ROWS, 16, WIDTH), BF16),
             pltpu.VMEM((ROWS, 16, WIDTH), BF16),
             pltpu.VMEM((HEADS, KEYS, WIDTH), BF16),
@@ -575,8 +590,10 @@
             pltpu.VMEM((SLOTS * GROUP, WIDTH), F32),
             pltpu.VMEM((SLOTS * GROUP, WIDTH), F32),
             pltpu.VMEM((SLOTS * GROUP, WIDTH), F32),
-            pltpu.VMEM((CTX, MSG, WIDTH), BF16),
-            pltpu.VMEM((CTX, MSG, WIDTH), BF16),
+            pltpu.VMEM((CTX, SLOTS, WIDTH), BF16),
+            pltpu.VMEM((CTX, SLOTS, WIDTH), BF16),
+            pltpu.VMEM((CTX, 1, WIDTH), F32),
+            pltpu.VMEM((CTX, 1, WIDTH), F32),
             pltpu.VMEM((HEADS * 16, ROWS), F32),
             pltpu.VMEM((HEADS, ROWS), F32),
             pltpu.VMEM((CTX, ROWS), F32),
@@ -587,7 +604,7 @@
             pltpu.VMEM((UNITS, LOCAL), BF16),
             pltpu.VMEM((256, LOCAL), BF16),
             pltpu.VMEM((16 * SLOTS, ROWS), BF16),
-            pltpu.VMEM((half, WIDTH), F32),
+            pltpu.VMEM((16, WIDTH), F32),
             pltpu.VMEM((8, ROWS), F32),
             pltpu.VMEM((WIDTH, ROWS), F32),
             pltpu.VMEM((NX, WIDTH + 16, ROWS), BF16),
@@ -606,7 +623,7 @@
             pltpu.VMEM((NX, 64, 256), BF16),
             dma(HEADS), dma(HEADS), pltpu.SemaphoreType.DMA,
             dma(2, 7), dma(2, 7), dma(2, 3), dma(2, 3), dma(4, 3), dma(4, 3), dma(4, 3, 4), dma(4, 3, 4), dma(4, 4), dma(4, 4),
-            dma(CTX), dma(CTX),
+            dma(CTX), dma(CTX), dma(CTX), dma(CTX), dma(3),
             dma(4), dma(3), dma(3),
             dma(2, 2), dma(2, 2), dma(2, 2, 3), dma(2, 2, 3), dma(2, 2, 7), dma(2, 2, 7),
             dma(2, 7), dma(2, 7), dma(2, 3), dma(2, 3), dma(2), dma(2),

time: 132 us -> 129 us (0.977)
  Pallas kernels: 131 us -> 128 us
    pallas_call x1, Pallas kernels: 129 us -> 127 us  [per_device(): pl.pallas_call(layer_kernel, out_shape=[jax.ShapeDtypeStruct((4, LOCAL),...]
where the time goes in v4:
time: 129 us
  Pallas kernels  128 us (99%)
    pallas_call x1, Pallas kernels, per_device(): pl.pallas_call(layer_kernel, out_shape=[jax.ShapeDtypeStruct((4, LOCAL),...  127 us

profile of v4, /device:TPU:1, one launch (start us, length us, event | category | flops | bytes accessed | tf_op | source)
XLA Modules:
  0.0 129.1 jit_solution(11529599147476720026)
XLA Ops:
  0.6 127.1 %layer.1 = (bf16[4,2048]{1,0:T(4,128)(2,1)}, bf16[4,2048]{1,0:T(4,128)(2,1)}) custom-call(bf16[4,16,128]{2,1,0:T(8,128)(2,1)} %bitcast.12, s32[8,16,256]{2,1,0:T(8,128)} %bitcast.11, bf16[4,2048]{1,0:T(4,128)(2,1)} %residual_ref.1, f32[1,2048]{1,0:T(1,128)} %bitcast.13, bf16[8,2048,128]{2,1,0:T(8,128)(2,1)} %bitcast.7, bf16[8,2048,128]{2,1,0:T(8,128)(2,1)} %bitcast.8, ...), custom_call_target="tpu_custom_call" | custom-call | tf_op jit(solution)/shard_map/layer/pallas_call | solution.py:577
  127.8 1.3 %hand_out.1 = (bf16[4,2048]{1,0:T(4,128)(2,1)}, bf16[4,2048]{1,0:T(4,128)(2,1)}) custom-call(bf16[4,2048]{1,0:T(4,128)(2,1)} %get-tuple-element.4.stream_in, bf16[4,2048]{1,0:T(4,128)(2,1)} %get-tuple-element.5.update_in), custom_call_target="tpu_custom_call" | custom-call | tf_op jit(solution)/shard_map/hand_out/pallas_call | solution.py:638

commit v5 on v4

--- a/solution.py
+++ b/solution.py
@@ -233,14 +233,14 @@
 
         lax.fori_loop(0, SLOTS // 8, pick, 0)
 
-        for b in range(2):
-            at = pl.ds(b * 256, 256)
+        for b in range(4):
+            at = pl.ds(b * 128, 128)
             s = dot(q32[at, :].astype(BF16), kbuf[h], 1, 1)
             top = (jnp.max(s, axis=1, keepdims=True) * SCALE).astype(BF16).astype(F32)
             p = jnp.exp2(s * SCALE - top)
             total = jnp.sum(p, axis=1, keepdims=True)
             o32[at, :] = dot(p.astype(BF16), vbuf[h], 1, 0)
-            lane = lax.broadcasted_iota(jnp.int32, (256, WIDTH), 1)
+            lane = lax.broadcasted_iota(jnp.int32, (128, WIDTH), 1)
             st32[at, :] = jnp.where(lane == 0, top, total)
 
         lane = lax.broadcasted_iota(jnp.int32, (SLOTS, WIDTH), 1)

time: 129 us -> 132 us (1.023)
  Pallas kernels: 128 us -> 131 us
    pallas_call x1, Pallas kernels: 127 us -> 129 us  [per_device(): pl.pallas_call(layer_kernel, out_shape=[jax.ShapeDtypeStruct((4, LOCAL),...]
where the time goes in v5:
time: 132 us; the launch traced here: 131 us
  Pallas kernels  131 us (99%)
    pallas_call x1, Pallas kernels, per_device(): pl.pallas_call(layer_kernel, out_shape=[jax.ShapeDtypeStruct((4, LOCAL),...  129 us

profile of v5, /device:TPU:1, one launch (start us, length us, event | category | flops | bytes accessed | tf_op | source)
XLA Modules:
  0.0 131.3 jit_solution(10409535024829018376)
XLA Ops:
  0.6 129.3 %layer.1 = (bf16[4,2048]{1,0:T(4,128)(2,1)}, bf16[4,2048]{1,0:T(4,128)(2,1)}) custom-call(bf16[4,16,128]{2,1,0:T(8,128)(2,1)} %bitcast.12, s32[8,16,256]{2,1,0:T(8,128)} %bitcast.11, bf16[4,2048]{1,0:T(4,128)(2,1)} %residual_ref.1, f32[1,2048]{1,0:T(1,128)} %bitcast.13, bf16[8,2048,128]{2,1,0:T(8,128)(2,1)} %bitcast.7, bf16[8,2048,128]{2,1,0:T(8,128)(2,1)} %bitcast.8, ...), custom_call_target="tpu_custom_call" | custom-call | tf_op jit(solution)/shard_map/layer/pallas_call | solution.py:577
  130.0 1.3 %hand_out.1 = (bf16[4,2048]{1,0:T(4,128)(2,1)}, bf16[4,2048]{1,0:T(4,128)(2,1)}) custom-call(bf16[4,2048]{1,0:T(4,128)(2,1)} %get-tuple-element.4.stream_in, bf16[4,2048]{1,0:T(4,128)(2,1)} %get-tuple-element.5.update_in), custom_call_target="tpu_custom_call" | custom-call | tf_op jit(solution)/shard_map/hand_out/pallas_call | solution.py:638

commit v6 on v5

--- a/solution.py
+++ b/solution.py
@@ -233,14 +233,14 @@
 
         lax.fori_loop(0, SLOTS // 8, pick, 0)
 
-        for b in range(4):
-            at = pl.ds(b * 128, 128)
+        for b in range(1):
+            at = pl.ds(b * 512, 512)
             s = dot(q32[at, :].astype(BF16), kbuf[h], 1, 1)
             top = (jnp.max(s, axis=1, keepdims=True) * SCALE).astype(BF16).astype(F32)
             p = jnp.exp2(s * SCALE - top)
             total = jnp.sum(p, axis=1, keepdims=True)
             o32[at, :] = dot(p.astype(BF16), vbuf[h], 1, 0)
-            lane = lax.broadcasted_iota(jnp.int32, (128, WIDTH), 1)
+            lane = lax.broadcasted_iota(jnp.int32, (512, WIDTH), 1)
             st32[at, :] = jnp.where(lane == 0, top, total)
 
         lane = lax.broadcasted_iota(jnp.int32, (SLOTS, WIDTH), 1)

time: 132 us -> 136 us (1.030)
  Pallas kernels: 131 us -> 135 us
    pallas_call x1, Pallas kernels: 129 us -> 134 us  [per_device(): pl.pallas_call(layer_kernel, out_shape=[jax.ShapeDtypeStruct((4, LOCAL),...]
where the time goes in v6:
time: 136 us
  Pallas kernels  135 us (99%)
    pallas_call x1, Pallas kernels, per_device(): pl.pallas_call(layer_kernel, out_shape=[jax.ShapeDtypeStruct((4, LOCAL),...  134 us

profile of v6, /device:TPU:1, one launch (start us, length us, event | category | flops | bytes accessed | tf_op | source)
XLA Modules:
  0.0 135.8 jit_solution(5609430798489869685)
XLA Ops:
  0.6 133.8 %layer.1 = (bf16[4,2048]{1,0:T(4,128)(2,1)}, bf16[4,2048]{1,0:T(4,128)(2,1)}) custom-call(bf16[4,16,128]{2,1,0:T(8,128)(2,1)} %bitcast.12, s32[8,16,256]{2,1,0:T(8,128)} %bitcast.11, bf16[4,2048]{1,0:T(4,128)(2,1)} %residual_ref.1, f32[1,2048]{1,0:T(1,128)} %bitcast.13, bf16[8,2048,128]{2,1,0:T(8,128)(2,1)} %bitcast.7, bf16[8,2048,128]{2,1,0:T(8,128)(2,1)} %bitcast.8, ...), custom_call_target="tpu_custom_call" | custom-call | tf_op jit(solution)/shard_map/layer/pallas_call | solution.py:577
  134.4 1.3 hand_out.1
